TPU v7x, 32 devices: a whole 2x2x4 slice. The times are simulated.
32 devices in a mesh: vox: 8 (over z, core), fsdp: 4 (over y, x).
Axes of the slice: x: 2, y: 2, z: 4, core: 2. Of those that a mesh axis runs over, the one named last changes fastest.
Arguments:
- tokens: bfloat16 [4, 3072, 1024], P('fsdp', 'vox'), may hold values from -6 to 6
- gain: float32 [1024], replicated, may hold values from 0.5 to 1.5
- w_qkv: bfloat16 [1024, 3072], P('fsdp'), may hold values from -0.1875 to 0.1875
- w_out: bfloat16 [1024, 1024], P('fsdp'), may hold values from -0.1875 to 0.1875
- logit_scale: float32 [16], replicated, may hold values from 4 to 240
- key_blocks: int32 [4, 48, 8], P('fsdp', 'vox'), may hold values from 0 to 47, as said below
- slot_count: int32 [4, 48], P('fsdp', 'vox'), may hold values from 1 to 8, as said below
- valid_voxels: int32 [4, 48], P('fsdp'), may hold values from 8 to 64
- cotangent: bfloat16 [4, 3072, 1024], P('fsdp', 'vox'), may hold values from -6 to 6
Outputs:
- mixed: bfloat16 [4, 3072, 1024], P('fsdp', 'vox')
- d_tokens: bfloat16 [4, 3072, 1024], P('fsdp', 'vox')
- d_wqkv: float32 [1024, 3072], P('fsdp', 'vox')
- d_wout: float32 [1024, 1024], P('fsdp', 'vox')
- d_gain: float32 [1024], replicated
- d_scale: float32 [16], replicated
Inputs may be any that keep to these rules, and one draw needn't show every extreme that they name: `key_blocks`: slot 0 of every block names the block itself; every listed block lies in the same scene within 3 blocks of its query block, and that distance is reached. Slots from slot_count on are not used.
All inputs are finite; a program needn't handle non-finite values.
Results may differ from a plain program's by a relative error of at most 0.012.
The roundings to bfloat16 on the way count: a program that leaves them out, or rounds other values in their place, can miss the bound.
Values may be sent and summed in bfloat16 or wider, within the bound.
No kernel may reach another device: no remote copies, remote signals or barrier semaphores. Data moves between devices by JAX's collectives and lax.ppermute only.
A program may use at most 128 MiB of HBM per device.

v0:
```python
import jax
import jax.numpy as jnp
from jax import lax
from jax.sharding import PartitionSpec as P

HEADS = 16
HD = 64


EPS = 1e-06


def padded(value, sides, width):
    for axis, dim in sides:
        count, length = (lax.axis_size(axis), value.shape[dim])
        up = [(i, (i + 1) % count) for i in range(count - 1)]
        down = [(j, i) for i, j in up]
        last = lax.slice_in_dim(value, length - width, length, axis=dim)
        first = lax.slice_in_dim(value, 0, width, axis=dim)
        before = lax.ppermute(last, axis, up)
        after = lax.ppermute(first, axis, down)
        value = jnp.concatenate([before, value, after], axis=dim)
    return value


def unit_rows(vectors):
    lengths = jnp.sqrt(jnp.sum(vectors * vectors, axis=-1, keepdims=True) + EPS)
    return (vectors / lengths, lengths)


def unit_back(unit, lengths, grads):
    return (grads - unit * jnp.sum(unit * grads, axis=-1, keepdims=True)) / lengths


def pair_heads(
    query_part,
    key_part,
    value_part,
    grad_part,
    scale_pair,
    slot_index,
    slot_mask,
    key_live,
    query_live,
):
    block_total, block_rows, pair_width = query_part.shape
    pool_size = key_part.shape[0]
    head_size = pair_width // 2
    query_unit, query_len = unit_rows(
        query_part.astype(jnp.float32).reshape(block_total, block_rows, 2, head_size)
    )
    key_unit, key_len = unit_rows(
        key_part.astype(jnp.float32).reshape(pool_size, block_rows, 2, head_size)
    )
    query_low = query_unit.astype(jnp.bfloat16)
    key_low = key_unit.astype(jnp.bfloat16)
    picked_keys = jnp.take(key_low, slot_index, axis=0)
    picked_values = jnp.take(
        value_part.reshape(pool_size, block_rows, 2, head_size), slot_index, axis=0
    )
    cosine = jnp.einsum(
        "bihd,bsjhd->bhisj", query_low, picked_keys, preferred_element_type=jnp.float32
    )
    allowed = jnp.logical_and(slot_mask[:, :, None], jnp.take(key_live, slot_index, axis=0))[
        :, None, None, :, :
    ]
    scale_view = scale_pair[None, :, None, None, None]
    scores = jnp.where(allowed, cosine * scale_view, -jnp.inf)
    row_peak = jnp.max(scores, axis=(3, 4), keepdims=True)
    raised = jnp.where(allowed, jnp.exp(scores - row_peak), 0.0)
    weights = raised / jnp.sum(raised, axis=(3, 4), keepdims=True)
    weights_low = weights.astype(jnp.bfloat16)
    row_keep = query_live[:, :, None, None]
    mixed_part = jnp.einsum(
        "bhisj,bsjhd->bihd", weights_low, picked_values, preferred_element_type=jnp.float32
    )
    mixed_part = jnp.where(row_keep, mixed_part, 0.0)
    upstream = jnp.where(
        row_keep,
        grad_part.reshape(block_total, block_rows, 2, head_size),
        jnp.zeros((), jnp.bfloat16),
    )
    weight_grad = jnp.einsum(
        "bihd,bsjhd->bhisj", upstream, picked_values, preferred_element_type=jnp.float32
    )
    value_term = jnp.einsum(
        "bhisj,bihd->bsjhd", weights_low, upstream, preferred_element_type=jnp.float32
    )
    centre = jnp.sum(weights * weight_grad, axis=(3, 4), keepdims=True)
    score_grad = weights * (weight_grad - centre)
    scale_grad = jnp.sum(score_grad * cosine, axis=(0, 2, 3, 4))
    cosine_grad = (score_grad * scale_view).astype(jnp.bfloat16)
    query_unit_grad = jnp.einsum(
        "bhisj,bsjhd->bihd", cosine_grad, picked_keys, preferred_element_type=jnp.float32
    )
    key_entry_grad = jnp.einsum(
        "bhisj,bihd->bsjhd", cosine_grad, query_low, preferred_element_type=jnp.float32
    )
    query_grad = unit_back(query_unit, query_len, query_unit_grad)
    empty_pool = jnp.zeros((pool_size, block_rows, 2, head_size), jnp.float32)
    key_unit_grad = empty_pool.at[slot_index].add(key_entry_grad)
    key_grad = unit_back(key_unit, key_len, key_unit_grad)
    value_grad = empty_pool.at[slot_index].add(value_term)
    return (
        mixed_part.reshape(block_total, block_rows, pair_width),
        query_grad.reshape(block_total, block_rows, pair_width),
        key_grad.reshape(pool_size, block_rows, pair_width),
        value_grad.reshape(pool_size, block_rows, pair_width),
        scale_grad,
    )


def merge_heads(stacked):
    pair_total, block_total, block_rows, pair_width = stacked.shape
    return jnp.transpose(stacked, (1, 2, 0, 3)).reshape(
        block_total * block_rows, pair_total * pair_width
    )


def on_device(
    tokens, gain, w_qkv, w_out, logit_scale, key_blocks, slot_count, valid_voxels, cotangent
):
    own_tokens = tokens[0]
    own_cotangent = cotangent[0]
    row_count, model_width = own_tokens.shape
    own_blocks = key_blocks.shape[1]
    slot_total = key_blocks.shape[2]
    block_rows = row_count // own_blocks
    reach_blocks = own_blocks // 2
    margin = reach_blocks * block_rows
    pool_size = own_blocks + 2 * reach_blocks
    pair_width = 2 * HD
    qkv_all, out_all = (
        lax.all_gather(w_qkv, "fsdp", axis=0, tiled=True),
        lax.all_gather(w_out, "fsdp", axis=0, tiled=True),
    )
    wide_tokens = own_tokens.astype(jnp.float32)
    inverse = lax.rsqrt(jnp.mean(wide_tokens * wide_tokens, axis=1, keepdims=True) + EPS)
    normed = (wide_tokens * inverse * gain).astype(jnp.bfloat16)
    packed = jnp.dot(normed, qkv_all, preferred_element_type=jnp.float32).astype(jnp.bfloat16)
    upstream_all = jnp.dot(own_cotangent, out_all.T, preferred_element_type=jnp.float32).astype(
        jnp.bfloat16
    )
    pool_rows = padded(packed[:, model_width:], (("vox", 0),), margin)
    pool_grid = pool_rows.reshape(pool_size, block_rows, 2 * model_width)
    query_grid = packed[:, :model_width].reshape(own_blocks, block_rows, model_width)
    upstream_grid = upstream_all.reshape(own_blocks, block_rows, model_width)
    first_block = lax.axis_index("vox") * own_blocks
    slot_index = key_blocks[0] - first_block + reach_blocks
    scene_total = valid_voxels.shape[1]
    pool_ids = first_block - reach_blocks + jnp.arange(pool_size, dtype=jnp.int32)
    pool_voxels = jnp.take(valid_voxels[0], jnp.clip(pool_ids, 0, scene_total - 1))
    key_live = jnp.arange(block_rows, dtype=jnp.int32)[None, :] < pool_voxels[:, None]
    query_live = key_live[reach_blocks : reach_blocks + own_blocks]
    slot_mask = jnp.arange(slot_total, dtype=jnp.int32)[None, :] < slot_count[0][:, None]

    def one_pair(pair_index):
        start = pair_index * pair_width
        query_part = lax.dynamic_slice_in_dim(query_grid, start, pair_width, 2)
        key_part = lax.dynamic_slice_in_dim(pool_grid, start, pair_width, 2)
        value_part = lax.dynamic_slice_in_dim(pool_grid, model_width + start, pair_width, 2)
        grad_part = lax.dynamic_slice_in_dim(upstream_grid, start, pair_width, 2)
        scale_pair = lax.dynamic_slice_in_dim(logit_scale, pair_index * 2, 2)
        return pair_heads(
            query_part,
            key_part,
            value_part,
            grad_part,
            scale_pair,
            slot_index,
            slot_mask,
            key_live,
            query_live,
        )

    outputs = lax.map(one_pair, jnp.arange(HEADS // 2, dtype=jnp.int32))
    attention = merge_heads(outputs[0]).astype(jnp.bfloat16)
    mixed = (wide_tokens + jnp.dot(attention, out_all, preferred_element_type=jnp.float32)).astype(
        jnp.bfloat16
    )
    out_grad = jnp.dot(attention.T, own_cotangent, preferred_element_type=jnp.float32)
    pool_grad = jnp.concatenate([merge_heads(outputs[2]), merge_heads(outputs[3])], axis=1)
    rim_grads = jnp.concatenate([pool_grad[:margin], pool_grad[margin + row_count :]], axis=0)
    returned = padded(rim_grads, (("vox", 0),), margin)
    kv_grad = pool_grad[margin : margin + row_count]
    kv_grad = kv_grad.at[:margin].add(returned[:margin])
    kv_grad = kv_grad.at[row_count - margin :].add(returned[3 * margin :])
    grad_packed = jnp.concatenate([merge_heads(outputs[1]), kv_grad], axis=1).astype(jnp.bfloat16)
    qkv_grad = jnp.dot(normed.T, grad_packed, preferred_element_type=jnp.float32)
    normed_grad = jnp.dot(grad_packed, qkv_all.T, preferred_element_type=jnp.float32)
    gain_grad = jnp.sum(normed_grad * wide_tokens * inverse, axis=0)
    scaled_grad = normed_grad * gain
    token_grad = own_cotangent.astype(jnp.float32) + inverse * (
        scaled_grad
        - wide_tokens
        * inverse
        * inverse
        * jnp.mean(scaled_grad * wide_tokens, axis=1, keepdims=True)
    )
    scale_grad = outputs[4].reshape(HEADS)
    part_qkv, part_out = (
        lax.psum_scatter(qkv_grad, "fsdp", scatter_dimension=0, tiled=True),
        lax.psum_scatter(out_grad, "fsdp", scatter_dimension=0, tiled=True),
    )
    summed_qkv, summed_out = (
        lax.psum_scatter(part_qkv, "vox", scatter_dimension=1, tiled=True),
        lax.psum_scatter(part_out, "vox", scatter_dimension=1, tiled=True),
    )
    summed_gain, summed_scale = lax.psum((gain_grad, scale_grad), ("vox", "fsdp"))
    return (
        mixed[None],
        token_grad.astype(jnp.bfloat16)[None],
        summed_qkv,
        summed_out,
        summed_gain,
        summed_scale,
    )


def solution(mesh):
    return jax.shard_map(
        on_device,
        mesh=mesh,
        in_specs=(
            P("fsdp", "vox", None),
            P(),
            P("fsdp", None),
            P("fsdp", None),
            P(),
            P("fsdp", "vox", None),
            P("fsdp", "vox"),
            P("fsdp", None),
            P("fsdp", "vox", None),
        ),
        out_specs=(
            P("fsdp", "vox", None),
            P("fsdp", "vox", None),
            P("fsdp", "vox"),
            P("fsdp", "vox"),
            P(),
            P(),
        ),
        check_vma=False,
    )
```

profile of v0, /device:TPU:0, one launch (start us, length us, event | category | flops | bytes accessed | tf_op | source)
XLA Modules:
  0.0 1117.9 jit_solution(12824699275848723321)
XLA Ops:
  9.7 73.1 %all-gather.3.cloned.1.call-done = bf16[1024,3072]{1,0:T(8,128)(2,1)} async-done(((bf16[256,3072]{1,0:T(8,128)(2,1)}), bf16[1024,3072]{1,0:T(8,128)(2,1)}) %all-gather.3.cloned.1.call-update) | async-done | bytes 6291472 | tf_op jit(solution)/shard_map/all_gather | solution.py:134
  82.8 5.8 convolution_convert_fusion
  94.7 25.3 %all-gather.5.cloned.1.call-done = bf16[1024,1024]{1,0:T(8,128)(2,1)} async-done(((bf16[256,1024]{1,0:T(8,128)(2,1)}), bf16[1024,1024]{1,0:T(8,128)(2,1)}) %all-gather.5.cloned.1.call-update) | async-done | bytes 2097168 | tf_op jit(solution)/shard_map/all_gather | solution.py:135
  128.1 723.7 %while.23 = (s32[]{:T(128)}, bf16[8,6,64,128]{2,3,1,0:T(8,128)(2,1)}, bf16[8,6,64,128]{2,3,1,0:T(8,128)(2,1)}, f32[8,12,64,128]{3,2,1,0:T(8,128)}, f32[8,12,64,1...) while((s32[]{:T(128)}, ...), condition=%wide.region_12.14_spmd.clone, body=%wide.region_1.13_spmd.clone.sunk | while | flops 315516416 | bytes 92074304 | solution.py:176
  169.5 6.7 scatter_fusion
  176.2 4.8 fusion.119
  194.5 9.9 scatter_fusion.1
  259.9 6.7 scatter_fusion
  266.6 4.8 fusion.119
  284.9 9.9 scatter_fusion.1
  350.3 6.7 scatter_fusion
  375.3 9.9 scatter_fusion.1
  440.7 6.7 scatter_fusion
  465.7 9.9 scatter_fusion.1
  531.1 6.7 scatter_fusion
  537.9 4.8 fusion.119
  556.2 9.9 scatter_fusion.1
  621.6 6.7 scatter_fusion
  628.3 4.8 fusion.119
  646.6 9.9 scatter_fusion.1
  712.1 6.7 scatter_fusion
  718.8 4.8 fusion.119
  737.1 9.9 scatter_fusion.1
  802.5 6.7 scatter_fusion
  809.3 4.8 fusion.119
  827.5 9.9 scatter_fusion.1
  881.1 6.7 fusion.50
  888.0 22.0 %reduce-scatter.9.cloned.1.call-done = f32[256,1024]{1,0:T(8,128)} async-done(((f32[1024,1024]{1,0:T(8,128)}), f32[256,1024]{1,0:T(8,128)}) %reduce-scatter.9.cloned.1.call-update) | async-done | bytes 1048592 | tf_op jit(solution)/shard_map/reduce_scatter | solution.py:203
  910.3 123.7 %reduce-scatter.5.cloned.1.call-done = f32[256,3072]{1,0:T(8,128)} async-done(((f32[1024,3072]{1,0:T(8,128)}), f32[256,3072]{1,0:T(8,128)}) %reduce-scatter.5.cloned.1.call-update) | async-done | bytes 3145744 | tf_op jit(solution)/shard_map/reduce_scatter | solution.py:202
  1037.8 5.8 fusion.47
  1043.6 39.5 %all-reduce = (f32[1024]{0:T(1024)}, f32[16]{0:T(128)}) all-reduce(f32[1024]{0:T(1024)S(1)} %get-tuple-element.350, f32[16]{0:T(128)S(1)} %reshape.241), channel_id=1, replica_groups=mesh['vox'=8,'fsdp'=4] {'vox','fsdp'}, use_global_device_ids=true, to_apply=%region_19.21 | all-reduce | flops 1040 | bytes 8320 | tf_op jit(solution)/shard_map/psum | solution.py:209
  1084.5 26.5 %reduce-scatter.7.cloned.1.call-done = f32[256,384]{1,0:T(8,128)} async-done(((f32[256,3072]{1,0:T(8,128)}), f32[256,384]{1,0:T(8,128)}) %reduce-scatter.7.cloned.1.call-update) | async-done | bytes 393232 | tf_op jit(solution)/shard_map/reduce_scatter | solution.py:206
  (1054 shorter events, 598.9 us)
Async XLA Ops:
  7.2 75.6 %copy-start.38 = (f32[1024]{0:T(1024)S(1)}, f32[1024]{0:T(1024)}, u32[]{:S(2)}) copy-start(f32[1024]{0:T(1024)} %param.18) | copy-start | bytes 12292
  7.2 75.6 %all-gather.3.cloned.1.call-start = ((), (), s32[]{:S(2)}) async-start(), calls=%async_computation.4 | async-start | bytes 7864320 | tf_op jit(solution)/shard_map/all_gather | solution.py:134
  7.9 112.0 %all-gather.5.cloned.1.call-start = ((), (), s32[]{:S(2)}) async-start(), calls=%async_computation.5 | async-start | bytes 2621440 | tf_op jit(solution)/shard_map/all_gather | solution.py:135
  8.7 901.3 %reduce-scatter.9.cloned.1.call-start = ((), (), s32[]{:S(2)}) async-start(), calls=%async_computation.8 | async-start | bytes 5242880 | tf_op jit(solution)/shard_map/reduce_scatter | solution.py:203
  9.7 78.9 %copy-start.46 = (f32[384]{0:T(512)}, f32[384]{0:T(512)S(1)}, u32[]{:S(2)}) copy-start(f32[384]{0:T(512)S(1)} %add_rsqrt_fusion) | copy-start | bytes 4612
  88.6 31.4 %copy-start.24 = (bf16[1,384,1024]{2,1,0:T(8,128)(2,1)S(1)}, bf16[1,384,1024]{2,1,0:T(8,128)(2,1)}, u32[]{:S(2)}) copy-start(bf16[1,384,1024]{2,1,0:T(8,128)(2,1)} %param.25) | copy-start | bytes 2359300
  89.9 34.7 %collective-permute-start = (bf16[192,2048]{1,0:T(8,128)(2,1)}, bf16[192,2048]{1,0:T(8,128)(2,1)}, u32[]{:S(2)}, u32[]{:S(2)}) collective-permute-start(bf16[192,2048]{1,0:T(8,128)(2,1)} %get-tuple-element.399), channel_id=1, source_target_pairs={{0,4},{4,8},{8,12},{12,16},{16,20},{20,24},{24,28},{1,5},{5,9},{9,... | collective-permute-start | bytes 2359304 | tf_op jit(solution)/shard_map/ppermute | solution.py:20
  92.6 32.0 %collective-permute-start.1 = (bf16[192,2048]{1,0:T(8,128)(2,1)}, bf16[192,2048]{1,0:T(8,128)(2,1)}, u32[]{:S(2)}, u32[]{:S(2)}) collective-permute-start(bf16[192,2048]{1,0:T(8,128)(2,1)} %get-tuple-element.400), channel_id=1, source_target_pairs={{4,0},{8,4},{12,8},{16,12},{20,16},{24,20},{28,24},{5,1},{9,5},{13... | collective-permute-start | bytes 2359304 | tf_op jit(solution)/shard_map/ppermute | solution.py:21
  128.1 15.3 %copy-start.49 = (s32[12]{0:T(128)}, s32[12]{0:T(128)S(1)}, u32[]{:S(2)}) copy-start(s32[12]{0:T(128)S(1)} %get-tuple-element.581) | copy-start | bytes 148 | tf_op jit(solution)/shard_map/while
  218.5 15.2 %copy-start.32 = (s32[6,8]{1,0:T(8,128)}, s32[6,8]{1,0:T(8,128)S(1)}, u32[]{:S(2)}) copy-start(s32[6,8]{1,0:T(8,128)S(1)} %get-tuple-element.576) | copy-start | bytes 580 | tf_op jit(solution)/shard_map/while
  218.5 15.3 %copy-start.49 = (s32[12]{0:T(128)}, s32[12]{0:T(128)S(1)}, u32[]{:S(2)}) copy-start(s32[12]{0:T(128)S(1)} %get-tuple-element.581) | copy-start | bytes 148 | tf_op jit(solution)/shard_map/while
  308.9 15.2 %copy-start.32 = (s32[6,8]{1,0:T(8,128)}, s32[6,8]{1,0:T(8,128)S(1)}, u32[]{:S(2)}) copy-start(s32[6,8]{1,0:T(8,128)S(1)} %get-tuple-element.576) | copy-start | bytes 580 | tf_op jit(solution)/shard_map/while
  308.9 15.3 %copy-start.49 = (s32[12]{0:T(128)}, s32[12]{0:T(128)S(1)}, u32[]{:S(2)}) copy-start(s32[12]{0:T(128)S(1)} %get-tuple-element.581) | copy-start | bytes 148 | tf_op jit(solution)/shard_map/while
  399.3 15.2 %copy-start.32 = (s32[6,8]{1,0:T(8,128)}, s32[6,8]{1,0:T(8,128)S(1)}, u32[]{:S(2)}) copy-start(s32[6,8]{1,0:T(8,128)S(1)} %get-tuple-element.576) | copy-start | bytes 580 | tf_op jit(solution)/shard_map/while
  399.3 15.3 %copy-start.49 = (s32[12]{0:T(128)}, s32[12]{0:T(128)S(1)}, u32[]{:S(2)}) copy-start(s32[12]{0:T(128)S(1)} %get-tuple-element.581) | copy-start | bytes 148 | tf_op jit(solution)/shard_map/while
  489.8 15.2 %copy-start.32 = (s32[6,8]{1,0:T(8,128)}, s32[6,8]{1,0:T(8,128)S(1)}, u32[]{:S(2)}) copy-start(s32[6,8]{1,0:T(8,128)S(1)} %get-tuple-element.576) | copy-start | bytes 580 | tf_op jit(solution)/shard_map/while
  489.8 15.3 %copy-start.49 = (s32[12]{0:T(128)}, s32[12]{0:T(128)S(1)}, u32[]{:S(2)}) copy-start(s32[12]{0:T(128)S(1)} %get-tuple-element.581) | copy-start | bytes 148 | tf_op jit(solution)/shard_map/while
  580.2 15.2 %copy-start.32 = (s32[6,8]{1,0:T(8,128)}, s32[6,8]{1,0:T(8,128)S(1)}, u32[]{:S(2)}) copy-start(s32[6,8]{1,0:T(8,128)S(1)} %get-tuple-element.576) | copy-start | bytes 580 | tf_op jit(solution)/shard_map/while
  580.2 15.3 %copy-start.49 = (s32[12]{0:T(128)}, s32[12]{0:T(128)S(1)}, u32[]{:S(2)}) copy-start(s32[12]{0:T(128)S(1)} %get-tuple-element.581) | copy-start | bytes 148 | tf_op jit(solution)/shard_map/while
  670.7 15.2 %copy-start.32 = (s32[6,8]{1,0:T(8,128)}, s32[6,8]{1,0:T(8,128)S(1)}, u32[]{:S(2)}) copy-start(s32[6,8]{1,0:T(8,128)S(1)} %get-tuple-element.576) | copy-start | bytes 580 | tf_op jit(solution)/shard_map/while
  670.7 15.3 %copy-start.49 = (s32[12]{0:T(128)}, s32[12]{0:T(128)S(1)}, u32[]{:S(2)}) copy-start(s32[12]{0:T(128)S(1)} %get-tuple-element.581) | copy-start | bytes 148 | tf_op jit(solution)/shard_map/while
  761.1 15.3 %copy-start.49 = (s32[12]{0:T(128)}, s32[12]{0:T(128)S(1)}, u32[]{:S(2)}) copy-start(s32[12]{0:T(128)S(1)} %get-tuple-element.581) | copy-start | bytes 148 | tf_op jit(solution)/shard_map/while
  857.0 177.0 %reduce-scatter.5.cloned.1.call-start = ((), (), s32[]{:S(2)}) async-start(), calls=%async_computation.6 | async-start | bytes 15728640 | tf_op jit(solution)/shard_map/reduce_scatter | solution.py:202
  866.9 8.3 collective-permute-start.2
  869.9 7.8 collective-permute-start.3
  887.9 146.1 %copy-start.53 = (f32[8,2]{1,0:T(8,128)S(1)}, f32[8,2]{1,0:T(8,128)}, u32[]{:S(2)}) copy-start(f32[8,2]{1,0:T(8,128)} %get-tuple-element.645) | copy-start | bytes 196
  887.9 146.2 %copy-start.15 = (bf16[1,384,1024]{2,1,0:T(8,128)(2,1)S(1)}, bf16[1,384,1024]{2,1,0:T(8,128)(2,1)}, u32[]{:S(2)}) copy-start(bf16[1,384,1024]{2,1,0:T(8,128)(2,1)} %param.17) | copy-start | bytes 2359300
  887.9 146.2 %copy-start.19 = (bf16[6,64,8,128]{3,2,1,0:T(8,128)(2,1)S(1)}, bf16[6,64,8,128]{3,2,1,0:T(8,128)(2,1)}, u32[]{:S(2)}) copy-start(bf16[6,64,8,128]{3,2,1,0:T(8,128)(2,1)} %copy-done.18) | copy-start | bytes 2359300
  887.9 196.6 %reduce-scatter.11.cloned.1.call-start = ((), (), s32[]{:S(2)}) async-start(), calls=%async_computation.9 | async-start | bytes 1179648 | tf_op jit(solution)/shard_map/reduce_scatter | solution.py:207
  910.0 201.0 %reduce-scatter.7.cloned.1.call-start = ((), (), s32[]{:S(2)}) async-start(), calls=%async_computation.7 | async-start | bytes 3538944 | tf_op jit(solution)/shard_map/reduce_scatter | solution.py:206
  1037.8 45.3 %copy-start.26 = (bf16[1,384,1024]{2,1,0:T(8,128)(2,1)S(1)}, bf16[1,384,1024]{2,1,0:T(8,128)(2,1)}, u32[]{:S(2)}) copy-start(bf16[1,384,1024]{2,1,0:T(8,128)(2,1)} %param.25) | copy-start | bytes 2359300
  1037.8 73.3 %copy-start.1 = (s32[1,48]{1,0:T(1,128)S(1)}, s32[1,48]{1,0:T(1,128)}, u32[]{:S(2)}) copy-start(s32[1,48]{1,0:T(1,128)} %param.24) | copy-start | bytes 580
  (259 other events, 861.2 us)
Sparse Core Ops, SparseCore 0:
  9.9 72.8 all-gather.2
  84.6 35.3 all-gather.4
  857.1 52.8 reduce-scatter.8
  913.2 120.7 reduce-scatter.4
  1036.8 32.5 reduce-scatter.10
  1072.2 38.7 reduce-scatter.6
where the time goes:
time: 1120 us
  local copies, waits for them, and re-layouts  352 us (31%)
  waiting for transfers between devices  272 us (24%)
  other arithmetic  266 us (24%)
  matrix products  151 us (13%)
  blocking collectives  39.5 us (4%)
  between operations  14.5 us (1%)
  loops' own time  14 us (1%)
    reduce_scatter x1, waiting for transfers between devices, on_device(): lax.psum_scatter(qkv_grad, 'fsdp', scatter_dimension=0, tiled=True)  124 us
    scatter-add x8, other arithmetic, pair_heads(): value_grad = empty_pool.at[slot_index].add(value_term)  79.5 us
    all_gather x1, waiting for transfers between devices, on_device(): lax.all_gather(w_qkv, 'fsdp', axis=0, tiled=True)  73.1 us
    scatter-add x8, other arithmetic, pair_heads(): key_unit_grad = empty_pool.at[slot_index].add(key_entry_grad)  53.8 us
    dynamic_update_slice x40, local copies, waits for them, and re-layouts, on_device(): outputs = lax.map(one_pair, jnp.arange(HEADS // 2, dtype=jnp.int32))  50.1 us
    while x16, matrix products  47.3 us
    psum x1, blocking collectives, on_device(): lax.psum((gain_grad, scale_grad), ('vox', 'fsdp'))  39.5 us
    mul x16, other arithmetic, unit_back(): unit * jnp.sum(unit * grads, axis=-1, keepdims=True)  39.4 us
  transfers between devices with their start and end apart: 10, of which 5 were waited for; matrix products, arithmetic and copies ran while one was open for 4% of the time, Pallas kernels for 0%

commit v1 on v0

v1 whole, which is shorter than its diff:
```python
import functools

import jax
import jax.numpy as jnp
from jax import lax
from jax.experimental import pallas as pl
from jax.experimental.pallas import tpu as pltpu
from jax.sharding import PartitionSpec as P

HEADS = 16
HD = 64
PAIR = 2 * HD
BLK = 64
WINDOW = 8
EPS = 1e-06
LOG2E = 1.4426950408889634
BF = jnp.bfloat16
F32 = jnp.float32


def dot(a, b, dims=((1,), (0,))):
    return lax.dot_general(a, b, (dims, ((), ())), preferred_element_type=F32)


def head_sums(x, same_head):
    high = x.astype(BF)
    low = (x - high.astype(F32)).astype(BF)
    return dot(high, same_head) + dot(low, same_head)


def unit_rows(x, same_head):
    length = jnp.sqrt(head_sums(x * x, same_head) + EPS)
    return x / length, length


def unit_back(unit, length, grad, same_head):
    return (grad - unit * head_sums(unit * grad, same_head)) / length


def attention_kernel(
    mult_ref, valid_ref, scale_ref,
    q_ref, k_ref, v_ref, kb_ref, vb_ref, ka_ref, va_ref, u_ref,
    att_ref, dq_ref, dk_ref, dv_ref, rim_b_ref, rim_a_ref, ds_ref,
    k_unit, k_len, k_low, k_turn, v_low, v_turn, mult, s_ref, g_ref, e_ref, w_low, c_low, dk, dv,
):
    rows = q_ref.shape[0]
    margin = kb_ref.shape[0]
    pool = rows + 2 * margin
    reach = margin // BLK
    steps = rows // PAIR
    span = WINDOW * BLK
    pair = pl.program_id(0)

    lane = lax.broadcasted_iota(jnp.int32, (BLK, PAIR), 1)
    row = lax.broadcasted_iota(jnp.int32, (BLK, PAIR), 0)
    head_a = lax.broadcasted_iota(jnp.int32, (PAIR, PAIR), 0) < HD
    head_b = lax.broadcasted_iota(jnp.int32, (PAIR, PAIR), 1) < HD
    same_head = jnp.where(head_a == head_b, 1.0, 0.0).astype(BF)
    first_lanes = head_b

    @pl.when(pair == 0)
    def _():
        for t in range(steps):
            for w in range(WINDOW):
                count = jnp.where(lane < BLK, mult_ref[2 * t, w], mult_ref[2 * t + 1, w])
                live = row < valid_ref[2 * t + w]
                mult[t, w * BLK : (w + 1) * BLK, :] = jnp.where(live, count, 0).astype(F32)

    def split_heads(x):
        return jnp.concatenate(
            [jnp.where(first_lanes, x, 0.0), jnp.where(first_lanes, 0.0, x)], axis=0
        ).astype(BF)

    for src_k, src_v, at, count in (
        (kb_ref, vb_ref, 0, margin), (k_ref, v_ref, margin, rows), (ka_ref, va_ref, margin + rows, margin)
    ):
        for part in range(0, count, 128 if count % 128 == 0 else 64):
            size = 128 if count % 128 == 0 else 64
            place = slice(at + part, at + part + size)
            unit, length = unit_rows(src_k[part : part + size, :].astype(F32), same_head)
            k_unit[place, :] = unit
            k_len[place, :] = length
            k_low[place, :] = unit.astype(BF)
            v_low[place, :] = src_v[part : part + size, :]
    for part in range(0, pool, 128):
        place = slice(part, part + 128)
        k_turn[:, place] = jnp.transpose(k_low[place, :].astype(F32)).astype(BF)
        v_turn[:, place] = jnp.transpose(v_low[place, :].astype(F32)).astype(BF)

    dk[...] = jnp.zeros_like(dk)
    dv[...] = jnp.zeros_like(dv)
    wide_lane = lax.broadcasted_iota(jnp.int32, (1, 2 * PAIR), 1)
    scale = jnp.where(wide_lane < PAIR, scale_ref[2 * pair], scale_ref[2 * pair + 1])
    ds = jnp.zeros((8, 2 * PAIR), F32)

    for t in range(steps):
        own = slice(t * PAIR, (t + 1) * PAIR)
        window = slice(t * PAIR, t * PAIR + span)
        q_unit, q_len = unit_rows(q_ref[own, :].astype(F32), same_head)
        q_split = split_heads(q_unit)
        live = jnp.concatenate(
            [row < valid_ref[2 * t + reach], row < valid_ref[2 * t + 1 + reach]], axis=0
        )
        u_split = split_heads(jnp.where(live, u_ref[own, :].astype(F32), 0.0))
        s_ref[...] = dot(k_low[window, :], q_split, ((1,), (1,)))
        g_ref[...] = dot(v_low[window, :], u_split, ((1,), (1,)))

        def mult_of(part):
            half = mult[t, part, :]
            return jnp.concatenate([half, half], axis=1)

        parts = [slice(i, i + 32) for i in range(0, span, 32)]
        peak = jnp.full((8, 2 * PAIR), -1e30, F32)
        stretch = scale * LOG2E
        for part in parts:
            raised = jnp.where(mult_of(part) > 0.0, s_ref[part, :] * stretch, -1e30)
            peak = jnp.maximum(peak, jnp.max(raised.reshape(4, 8, 2 * PAIR), axis=0))
        peak = jnp.max(peak, axis=0, keepdims=True)
        total = jnp.zeros((8, 2 * PAIR), F32)
        centre = jnp.zeros((8, 2 * PAIR), F32)
        for part in parts:
            count = mult_of(part)
            shifted = jnp.where(count > 0.0, s_ref[part, :] * stretch - peak, -1e30)
            e = jnp.exp2(shifted) * count
            e_ref[part, :] = e
            total = total + jnp.sum(e.reshape(4, 8, 2 * PAIR), axis=0)
            centre = centre + jnp.sum((e * g_ref[part, :]).reshape(4, 8, 2 * PAIR), axis=0)
        share = 1.0 / jnp.sum(total, axis=0, keepdims=True)
        centre = jnp.sum(centre, axis=0, keepdims=True) * share
        for part in parts:
            w = e_ref[part, :] * share
            w_low[part, :] = w.astype(BF)
            sg = w * (g_ref[part, :] - centre)
            ds = ds + jnp.sum((sg * s_ref[part, :]).reshape(4, 8, 2 * PAIR), axis=0)
            c_low[part, :] = (sg * scale).astype(BF)

        def by_query(turned):
            return jnp.transpose(
                jnp.concatenate([turned[:HD, :PAIR], turned[HD:, PAIR:]], axis=0)
            )

        mixed = by_query(dot(v_turn[:, window], w_low[...]))
        att_ref[own, :] = jnp.where(live, mixed, 0.0).astype(BF)
        q_grad = by_query(dot(k_turn[:, window], c_low[...]))
        dq_ref[own, :] = unit_back(q_unit, q_len, q_grad, same_head).astype(BF)
        dv[window, :] += dot(w_low[...], u_split)
        dk[window, :] += dot(c_low[...], q_split)

    for part in range(0, pool, 64):
        place = slice(part, part + 64)
        grad_k = unit_back(k_unit[place, :], k_len[place, :], dk[place, :], same_head)
        grad_v = dv[place, :]
        if part < margin:
            rim_b_ref[0, place, :] = grad_k
            rim_b_ref[1, place, :] = grad_v
        elif part < margin + rows:
            here = slice(part - margin, part - margin + 64)
            dk_ref[here, :] = grad_k
            dv_ref[here, :] = grad_v
        else:
            here = slice(part - margin - rows, part - margin - rows + 64)
            rim_a_ref[0, here, :] = grad_k
            rim_a_ref[1, here, :] = grad_v
    ds_ref[0, :, :] = ds


def attention(packed, before, after, upstream, mult, valid, scales):
    rows, width3 = packed.shape
    width = width3 // 3
    margin = before.shape[0]
    pool = rows + 2 * margin
    pairs = width // PAIR
    steps = rows // PAIR
    span = WINDOW * BLK

    def at(offset):
        return lambda p, *_: (0, offset + p)

    return pl.pallas_call(
        attention_kernel,
        grid_spec=pltpu.PrefetchScalarGridSpec(
            num_scalar_prefetch=3,
            grid=(pairs,),
            in_specs=[
                pl.BlockSpec((rows, PAIR), at(0)),
                pl.BlockSpec((rows, PAIR), at(pairs)),
                pl.BlockSpec((rows, PAIR), at(2 * pairs)),
                pl.BlockSpec((margin, PAIR), at(0)),
                pl.BlockSpec((margin, PAIR), at(pairs)),
                pl.BlockSpec((margin, PAIR), at(0)),
                pl.BlockSpec((margin, PAIR), at(pairs)),
                pl.BlockSpec((rows, PAIR), at(0)),
            ],
            out_specs=[
                pl.BlockSpec((rows, PAIR), at(0)),
                pl.BlockSpec((rows, PAIR), at(0)),
                pl.BlockSpec((rows, PAIR), at(0)),
                pl.BlockSpec((rows, PAIR), at(0)),
                pl.BlockSpec((2, margin, PAIR), lambda p, *_: (0, 0, p)),
                pl.BlockSpec((2, margin, PAIR), lambda p, *_: (0, 0, p)),
                pl.BlockSpec((1, 8, 2 * PAIR), lambda p, *_: (p, 0, 0)),
            ],
            scratch_shapes=[
                pltpu.VMEM((pool, PAIR), F32),
                pltpu.VMEM((pool, PAIR), F32),
                pltpu.VMEM((pool, PAIR), BF),
                pltpu.VMEM((PAIR, pool), BF),
                pltpu.VMEM((pool, PAIR), BF),
                pltpu.VMEM((PAIR, pool), BF),
                pltpu.VMEM((steps, span, PAIR), F32),
                pltpu.VMEM((span, 2 * PAIR), F32),
                pltpu.VMEM((span, 2 * PAIR), F32),
                pltpu.VMEM((span, 2 * PAIR), F32),
                pltpu.VMEM((span, 2 * PAIR), BF),
                pltpu.VMEM((span, 2 * PAIR), BF),
                pltpu.VMEM((pool, PAIR), F32),
                pltpu.VMEM((pool, PAIR), F32),
            ],
        ),
        out_shape=[
            jax.ShapeDtypeStruct((rows, width), BF),
            jax.ShapeDtypeStruct((rows, width), BF),
            jax.ShapeDtypeStruct((rows, width), F32),
            jax.ShapeDtypeStruct((rows, width), F32),
            jax.ShapeDtypeStruct((2, margin, width), F32),
            jax.ShapeDtypeStruct((2, margin, width), F32),
            jax.ShapeDtypeStruct((pairs, 8, 2 * PAIR), F32),
        ],
        compiler_params=pltpu.CompilerParams(vmem_limit_bytes=40 * 1024 * 1024),
        cost_estimate=pl.CostEstimate(
            flops=2 * 6 * pairs * steps * span * 256 * 128,
            bytes_accessed=packed.size * 2 + rows * width * 14,
            transcendentals=pairs * steps * span * 256,
        ),
        name="block_attention",
    )(mult, valid, scales, packed, packed, packed, before, before, after, after, upstream)


def pick_groups(array, axis, unit, core):
    shape = array.shape
    split = shape[:axis] + (shape[axis] // (2 * unit), 2, unit) + shape[axis + 1 :]
    picked = lax.dynamic_index_in_dim(array.reshape(split), core, axis + 1, keepdims=False)
    return picked.reshape(shape[:axis] + (shape[axis] // 2,) + shape[axis + 1 :])


def in_order(core, own, other, axis):
    first = jnp.where(core == 0, own, other)
    second = jnp.where(core == 0, other, own)
    return jnp.concatenate([first, second], axis=axis)


def on_device(
    tokens, gain, w_qkv, w_out, logit_scale, key_blocks, slot_count, valid_voxels, cotangent
):
    own_tokens = tokens[0]
    own_cotangent = cotangent[0]
    own_rows, model_width = own_tokens.shape
    rows = 2 * own_rows
    own_blocks = key_blocks.shape[1]
    blocks = 2 * own_blocks
    slot_total = key_blocks.shape[2]
    reach = own_blocks // 2
    margin = reach * BLK
    n_vox = lax.axis_size("vox")
    n_chip = n_vox // 2
    place = lax.axis_index("vox")
    core = place % 2
    chip = place // 2
    chip_columns = 3 * model_width // n_chip
    unit = 128 if chip_columns % 256 == 0 and w_out.shape[0] % 256 == 0 else 64
    swap = [(i, i ^ 1) for i in range(n_vox)]
    up = [(i, i + 2) for i in range(n_vox - 2)]
    down = [(j, i) for i, j in up]
    same_core = [[2 * i + c for i in range(n_chip)] for c in range(2)]

    qkv_half = lax.all_gather(pick_groups(w_qkv, 1, unit, core), "fsdp", axis=0, tiled=True)
    out_half = lax.all_gather(pick_groups(w_out, 0, unit, core), "fsdp", axis=0, tiled=True)

    other_tokens = lax.ppermute(own_tokens, "vox", swap)
    other_cotangent = lax.ppermute(own_cotangent, "vox", swap)
    lists = jnp.concatenate([key_blocks[0], slot_count[0][:, None]], axis=1)
    all_lists = in_order(
        core, lists, lax.ppermute(lists.astype(F32), "vox", swap).astype(jnp.int32), 0
    )
    chip_tokens = in_order(core, own_tokens, other_tokens, 0)
    chip_cotangent = in_order(core, own_cotangent, other_cotangent, 0)

    first_block = chip * blocks
    pool_blocks = blocks + 2 * reach
    window_id = (
        all_lists[:, :slot_total] - first_block + reach
        - 2 * (jnp.arange(blocks, dtype=jnp.int32) // 2)[:, None]
    )
    used = jnp.arange(slot_total, dtype=jnp.int32)[None, :] < all_lists[:, slot_total:]
    hits = jnp.logical_and(
        window_id[:, :, None] == jnp.arange(WINDOW, dtype=jnp.int32), used[:, :, None]
    )
    mult = jnp.sum(hits.astype(jnp.int32), axis=1)
    scene_total = valid_voxels.shape[1]
    pool_ids = first_block - reach + jnp.arange(pool_blocks, dtype=jnp.int32)
    valid = jnp.take(valid_voxels[0], jnp.clip(pool_ids, 0, scene_total - 1))
    scales = pick_groups(logit_scale, 0, unit // HD, core)

    wide = chip_tokens.astype(F32)
    inverse = lax.rsqrt(jnp.mean(wide * wide, axis=1, keepdims=True) + EPS)
    normed = (wide * inverse * gain).astype(BF)
    packed = dot(normed, qkv_half).astype(BF)
    width = packed.shape[1] // 3
    before = lax.ppermute(packed[rows - margin :, width:], "vox", up)
    after = lax.ppermute(packed[:margin, width:], "vox", down)
    upstream = dot(chip_cotangent, out_half, ((1,), (1,))).astype(BF)

    att, dq, dk, dv, rim_b, rim_a, ds = attention(
        packed, before, after, upstream, mult, valid, scales
    )
    back_a = lax.ppermute(rim_b, "vox", down)
    back_b = lax.ppermute(rim_a, "vox", up)

    out_grad = dot(att, chip_cotangent, ((0,), (0,)))
    mixed_part = dot(att, out_half)
    mixed_mine = lax.dynamic_slice_in_dim(mixed_part, core * own_rows, own_rows, 0)
    mixed_theirs = lax.dynamic_slice_in_dim(mixed_part, (1 - core) * own_rows, own_rows, 0)
    mixed = (
        own_tokens.astype(F32) + (mixed_mine + lax.ppermute(mixed_theirs, "vox", swap))
    ).astype(BF)

    def with_rims(grad, index):
        return jnp.concatenate(
            [
                grad[:margin] + back_b[index],
                grad[margin : rows - margin],
                grad[rows - margin :] + back_a[index],
            ],
            axis=0,
        ).astype(BF)

    grad_packed = jnp.concatenate([dq, with_rims(dk, 0), with_rims(dv, 1)], axis=1)
    qkv_grad = dot(normed, grad_packed, ((0,), (0,)))
    ngrad_part = dot(grad_packed, qkv_half, ((1,), (1,)))
    ngrad_mine = lax.dynamic_slice_in_dim(ngrad_part, core * own_rows, own_rows, 0)
    ngrad_theirs = lax.dynamic_slice_in_dim(ngrad_part, (1 - core) * own_rows, own_rows, 0)
    normed_grad = ngrad_mine + lax.ppermute(ngrad_theirs, "vox", swap)

    own_wide = own_tokens.astype(F32)
    own_inverse = lax.rsqrt(jnp.mean(own_wide * own_wide, axis=1, keepdims=True) + EPS)
    gain_grad = jnp.sum(normed_grad * own_wide * own_inverse, axis=0)
    scaled_grad = normed_grad * gain
    token_grad = own_cotangent.astype(F32) + own_inverse * (
        scaled_grad
        - own_wide
        * own_inverse
        * own_inverse
        * jnp.mean(scaled_grad * own_wide, axis=1, keepdims=True)
    )

    group_heads = unit // HD
    scale_part = jnp.sum(ds.reshape(-1, 8, 2, PAIR), axis=(1, 3)).reshape(-1, 1, group_heads)
    mine = (jnp.arange(2) == core)[None, :, None]
    scale_grad = jnp.where(mine, scale_part, 0.0).reshape(HEADS)
    summed_gain, summed_scale = lax.psum((gain_grad, scale_grad), ("vox", "fsdp"))

    out_part = lax.psum_scatter(
        out_grad.astype(BF), "fsdp", scatter_dimension=0, tiled=True
    )
    out_sum = lax.psum_scatter(
        out_part, "vox", scatter_dimension=1, tiled=True, axis_index_groups=same_core
    ).astype(F32)
    qkv_part = lax.psum_scatter(
        qkv_grad.astype(BF), "fsdp", scatter_dimension=0, tiled=True
    )
    qkv_sum = lax.psum_scatter(
        qkv_part, "vox", scatter_dimension=1, tiled=True, axis_index_groups=same_core
    ).astype(F32)

    half = out_sum.shape[1] // 2
    out_mine = lax.dynamic_slice_in_dim(out_sum, core * half, half, 1)
    out_theirs = lax.ppermute(
        lax.dynamic_slice_in_dim(out_sum, (1 - core) * half, half, 1), "vox", swap
    )
    sets = out_sum.shape[0] // unit
    out_both = in_order(
        core,
        out_mine.reshape(sets, 1, unit, half),
        out_theirs.reshape(sets, 1, unit, half),
        1,
    )
    summed_out = out_both.reshape(2 * sets * unit, half)

    height, held = qkv_sum.shape
    qkv_other = lax.ppermute(qkv_sum, "vox", swap)
    qkv_both = in_order(
        core,
        qkv_sum.reshape(height, held // unit, 1, unit),
        qkv_other.reshape(height, held // unit, 1, unit),
        2,
    ).reshape(height, 2 * held)
    summed_qkv = lax.dynamic_slice_in_dim(qkv_both, core * held, held, 1)

    return (
        mixed[None],
        token_grad.astype(BF)[None],
        summed_qkv,
        summed_out,
        summed_gain,
        summed_scale,
    )


def solution(mesh):
    return jax.shard_map(
        on_device,
        mesh=mesh,
        in_specs=(
            P("fsdp", "vox", None),
            P(),
            P("fsdp", None),
            P("fsdp", None),
            P(),
            P("fsdp", "vox", None),
            P("fsdp", "vox"),
            P("fsdp", None),
            P("fsdp", "vox", None),
        ),
        out_specs=(
            P("fsdp", "vox", None),
            P("fsdp", "vox", None),
            P("fsdp", "vox"),
            P("fsdp", "vox"),
            P(),
            P(),
        ),
        check_vma=False,
    )
```

time: 1120 us -> 301 us (0.27)
  local copies, waits for them, and re-layouts: 352 us -> 25.2 us
  other arithmetic: 266 us -> 16.3 us
  waiting for transfers between devices: 272 us -> 142 us
  matrix products: 151 us -> 21.3 us
  Pallas kernels: 0 us -> 30.5 us
  loops' own time: 14 us -> 0 us
    scatter-add x18 -> x0, other arithmetic: 138 us -> none  [the longest x8 79.5 us: pair_heads(): value_grad = empty_pool.at[slot_index].add(value_term)]
    reduce_scatter x4 -> x3, waiting for transfers between devices: 172 us -> 44.4 us  [the longest x1 32.8 us: on_device(): lax.psum_scatter(qkv_grad.astype(BF), 'fsdp', scatter_dimension=0, tiled=...]
    dot_general x38 -> x6, matrix products: 103 us -> 21.3 us  [dot(): return lax.dot_general(a, b, (dims, ((), ())), preferred_element_type=F32)]
    transpose x19 -> x0, local copies, waits for them, and re-layouts: 54.9 us -> none  [the longest x8 28.7 us: pair_heads(): jnp.einsum('bhisj,bihd->bsjhd', weights_low, upstream, preferred_element_...]
    gather x33 -> x1, local copies, waits for them, and re-layouts: 52.9 us -> 0.7 us  [on_device(): valid = jnp.take(valid_voxels[0], jnp.clip(pool_ids, 0, scene_total - 1))]
    dynamic_update_slice x40 -> x0, local copies, waits for them, and re-layouts: 50.1 us -> none  [on_device(): outputs = lax.map(one_pair, jnp.arange(HEADS // 2, dtype=jnp.int32))]
    while x16 -> x0, matrix products: 47.3 us -> none
    all_gather x2, waiting for transfers between devices: 98.4 us -> 55.8 us  [the longest x1 41.4 us: on_device(): lax.all_gather(pick_groups(w_qkv, 1, unit, core), 'fsdp', axis=0, tiled=T...]
  transfers between devices with their start and end apart: 10 -> 17, of which waited for: 5 -> 7; matrix products, arithmetic and copies ran while one was open for 4% -> 15% of each run, Pallas kernels for 0% -> 0%
where the time goes in v1:
time: 301 us; the launch traced here: 300 us
  waiting for transfers between devices  142 us (47%)
  blocking collectives  38.7 us (13%)
  Pallas kernels  30.5 us (10%)
  local copies, waits for them, and re-layouts  25.2 us (8%)
  matrix products  21.3 us (7%)
  other arithmetic  16.3 us (5%)
  between operations  14.6 us (5%)
  starting transfers between devices  11.3 us (4%)
    all_gather x1, waiting for transfers between devices, on_device(): lax.all_gather(pick_groups(w_qkv, 1, unit, core), 'fsdp', axis=0, tiled=T...  41.4 us
    psum x1, blocking collectives, on_device(): lax.psum((gain_grad, scale_grad), ('vox', 'fsdp'))  38.7 us
    reduce_scatter x1, waiting for transfers between devices, on_device(): lax.psum_scatter(qkv_grad.astype(BF), 'fsdp', scatter_dimension=0, tiled=...  32.8 us
    pallas_call x1, Pallas kernels, attention(): pl.pallas_call(attention_kernel, grid_spec=pltpu.PrefetchScalarGridSpec(n...  30.5 us
    unnamed x7, waiting for transfers between devices  23.4 us
    dot_general x6, matrix products, dot(): return lax.dot_general(a, b, (dims, ((), ())), preferred_element_type=F32)  21.3 us
    unnamed x77, local copies, waits for them, and re-layouts  16 us
    ppermute x1, waiting for transfers between devices, on_device(): back_b = lax.ppermute(rim_a, 'vox', up)  14.4 us
  transfers between devices with their start and end apart: 17, of which 7 were waited for; matrix products, arithmetic and copies ran while one was open for 15% of the time, Pallas kernels for 0%

profile of v1, /device:TPU:0, one launch (start us, length us, event | category | flops | bytes accessed | tf_op | source)
XLA Modules:
  0.0 300.1 jit_solution(7710022838220270382)
XLA Ops:
  7.3 1.8 copy.40
  13.4 1.2 broadcast_select_fusion.3
  15.5 41.4 %all-gather.4.cloned.1.call-done = bf16[1024,1536]{0,1:T(8,128)(2,1)} async-done(((bf16[256,1536]{0,1:T(8,128)(2,1)}), bf16[1024,1536]{0,1:T(8,128)(2,1)}) %all-gather.4.cloned.1.call-update) | async-done | bytes 3145744 | tf_op jit(solution)/shard_map/all_gather | solution.py:276
  57.0 4.9 %convolution_convert_fusion.1.q_ref.k_ref.v_ref = bf16[768,1536]{1,0:T(8,128)(2,1)S(1)} fusion(bf16[1024,1536]{0,1:T(8,128)(2,1)} %all-gather.4.cloned.1.call-done, f32[1024]{0:T(1024)S(1)} %copy-done.33, f32[768]{0:T(1024)S(1)} %add_rsqrt_fusion, bf16[384,1024]{1,0:T(8,128)(2,1)} %copy-done.19, bf16[384,1024]{1,0:T(8,128)(2,1)S(1)} %get-tuple-element.59), kind=kOutput, calls=%fused_computation.4 | convolution fusion | flops 2422603776 | bytes 7085056 | tf_op jit(solution)/shard_map/dot_general | solution.py:22
  62.7 1.4 copy-done.2
  64.1 3.4 %collective-permute-start.2 = (bf16[192,1024]{1,0:T(8,128)(2,1)}, bf16[192,1024]{1,0:T(8,128)(2,1)S(1)}, u32[]{:S(2)}, u32[]{:S(2)}) collective-permute-start(bf16[192,1024]{1,0:T(8,128)(2,1)} %get-tuple-element.50), channel_id=1, source_target_pairs={{0,8},{4,12},{8,16},{12,20},{16,24},{20,28},{1,9},{5,13},{9,17},{1... | collective-permute-start | bytes 1179656 | tf_op jit(solution)/shard_map/ppermute | solution.py:309
  67.5 1.5 collective-permute-start.3
  69.0 2.1 broadcast_select_fusion.1
  71.2 14.3 %all-gather.6.cloned.1.call-done = bf16[1,1,512,1024]{3,2,1,0:T(8,128)(2,1)} async-done(((bf16[1,1,128,1024]{3,2,1,0:T(8,128)(2,1)}), bf16[1,1,512,1024]{3,2,1,0:T(8,128)(2,1)}) %all-gather.6.cloned.1.call-update) | async-done | bytes 1048592 | tf_op jit(solution)/shard_map/all_gather | solution.py:277
  85.5 2.6 convolution_convert_fusion.3.u_ref
  88.9 1.0 copy-done.7
  89.9 30.5 %block_attention.1 = (bf16[768,512]{1,0:T(8,128)(2,1)S(1)}, bf16[768,512]{1,0:T(8,128)(2,1)S(1)}, f32[768,512]{1,0:T(8,128)S(1)}, f32[768,512]{1,0:T(8,128)S(1)}...) custom-call(s32[12,8]{1,0:T(8,128)S(1)} %copy.41.mult_ref, ...), custom_call_target="tpu_custom_call" | custom-call | flops 4831838208 | bytes 7864320 | tf_op jit(solution)/shard_map/block_attention/pallas_call | solution.py:179
  120.4 1.1 copy-done.1
  124.2 2.0 convolution_convert_fusion.2
  126.3 3.5 %collective-permute-start.6 = (f32[2,192,512]{2,1,0:T(8,128)}, f32[2,192,512]{2,1,0:T(8,128)S(1)}, u32[]{:S(2)}, u32[]{:S(2)}) collective-permute-start(f32[2,192,512]{2,1,0:T(8,128)} %copy-done.5), channel_id=1, source_target_pairs={{0,8},{4,12},{8,16},{12,20},{16,24},{20,28},{1,9},{5,13},{9,17},{1... | collective-permute-start | bytes 2359304 | tf_op jit(solution)/shard_map/ppermute | solution.py:317
  129.8 1.3 collective-permute-start.7
  131.1 1.2 slice.111
  132.4 14.4 %collective-permute-done.6 = f32[2,192,512]{2,1,0:T(8,128)S(1)} collective-permute-done((f32[2,192,512]{2,1,0:T(8,128)}, f32[2,192,512]{2,1,0:T(8,128)S(1)}, u32[]{:S(2)}, u32[]{:S(2)}) %collective-permute-start.6) | collective-permute-done | bytes 786464 | tf_op jit(solution)/shard_map/ppermute | solution.py:317
  146.8 4.1 %collective-permute-done.7 = f32[2,192,512]{2,1,0:T(8,128)S(1)} collective-permute-done((f32[2,192,512]{2,1,0:T(8,128)}, f32[2,192,512]{2,1,0:T(8,128)S(1)}, u32[]{:S(2)}, u32[]{:S(2)}) %collective-permute-start.7) | collective-permute-done | bytes 786464 | tf_op jit(solution)/shard_map/ppermute | solution.py:316
  150.9 1.4 fusion.22
  153.1 4.6 %convolution_convert_fusion = bf16[1024,1536]{1,0:T(8,128)(2,1)} fusion(f32[1024]{0:T(1024)S(1)} %copy-done.33, f32[768]{0:T(1024)S(1)} %add_rsqrt_fusion, bf16[384,1024]{1,0:T(8,128)(2,1)S(1)} %copy-done.20, bf16[384,1024]{1,0:T(8,128)(2,1)S(1)} %copy-done.18, bf16[192,512]{1,0:T(8,128)(2,1)S(1)} %get-tuple-element.54, bf16[384,512]{1,0:T(8,128)(2,1)S(1)} %slice.111, ...), kind=kOutput, calls=%fused_computation.3 | convolution fusion | flops 2439512064 | bytes 7085056 | tf_op jit(solution)/shard_map/dot_general | solution.py:22
  159.0 6.3 %fusion.45 = f32[768,1024]{1,0:T(8,128)} fusion(bf16[1024,1536]{0,1:T(8,128)(2,1)} %all-gather.4.cloned.1.call-done, bf16[192,512]{1,0:T(8,128)(2,1)S(1)} %copy-done.29, bf16[384,512]{1,0:T(8,128)(2,1)S(1)} %slice.111, bf16[192,512]{1,0:T(8,128)(2,1)S(1)} %get-tuple-element.53, bf16[192,512]{1,0:T(8,128)(2,1)S(1)} %copy-done.31, ...), kind=kOutput, calls=%fused_computation.102 | convolution fusion | flops 2432434176 | bytes 8650752 | tf_op jit(solution)/shard_map/dot_general | solution.py:22
  165.3 2.8 constant_dynamic-slice_fusion.2
  168.4 32.8 %reduce-scatter.7.cloned.1.call-done = bf16[256,1536]{1,0:T(8,128)(2,1)} async-done(((bf16[1024,1536]{1,0:T(8,128)(2,1)}), bf16[256,1536]{1,0:T(8,128)(2,1)}) %reduce-scatter.7.cloned.1.call-update) | async-done | bytes 786448 | tf_op jit(solution)/shard_map/reduce_scatter | solution.py:368
  201.2 2.3 copy.47
  204.5 1.6 copy-done.12
  206.1 1.2 constant_dynamic-slice_fusion.3
  207.8 3.7 %fusion.13 = (f32[1024]{0:T(1024)S(1)}, f32[384]{0:T(512)S(1)}, f32[384,1024]{1,0:T(8,128)}) fusion(f32[384]{0:T(512)S(1)} %add_rsqrt_fusion.1, bf16[1,384,1024]{2,1,0:T(8,128)(2,1)S(1)} %copy-done.14, f32[1024]{0:T(1024)S(1)} %copy-done.33, f32[384,1024]{1,0:T(8,128)} %collective-permute-done.8, f32[768,1024]{1,0:T(8,128)} %fusion.45, s32[]{:T(128)S(6)} %select_n.170), kind=kLoop, calls=%fused_computation.24 | loop fusion | flops 3144320 | bytes 5516292 | tf_op jit(solution)/shard_map/reduce_sum | solution.py:346
  211.5 11.7 %reduce-scatter.11.cloned.1.call-done = bf16[128,256]{1,0:T(8,128)(2,1)} async-done(((bf16[128,1024]{1,0:T(8,128)(2,1)}), bf16[128,256]{1,0:T(8,128)(2,1)}) %reduce-scatter.11.cloned.1.call-update) | async-done | bytes 65552 | tf_op jit(solution)/shard_map/reduce_scatter | solution.py:365
  224.1 23.3 %reduce-scatter.13.cloned.1.call-done = bf16[384,256]{1,0:T(8,128)(2,1)} async-done(((bf16[1536,256]{1,0:T(8,128)(2,1)}), bf16[384,256]{1,0:T(8,128)(2,1)}) %reduce-scatter.13.cloned.1.call-update) | async-done | bytes 196624
  248.5 4.2 %fusion.17 = (bf16[1,384,1024]{2,1,0:T(8,128)(2,1)}, bf16[1,384,1024]{2,1,0:T(8,128)(2,1)}) fusion(f32[384,1024]{1,0:T(8,128)} %get-tuple-element.48, f32[384]{0:T(512)S(1)} %broadcast_multiply_fusion, f32[1024]{0:T(1024)S(1)} %copy-done.33, f32[384]{0:T(512)S(1)} %add_rsqrt_fusion.1, bf16[1,384,1024]{2,1,0:T(8,128)(2,1)S(1)} %copy-done.16, ...), kind=kLoop, calls=%fused_computation.33 | loop fusion | flops 5111808 | bytes 7871492 | tf_op jit(solution)/shard_map/broadcast_in_dim | solution.py:401
  252.7 38.7 %all-reduce = (f32[1024]{0:T(1024)}, f32[16]{0:T(128)}) all-reduce(f32[1024]{0:T(1024)S(1)} %get-tuple-element.44, f32[16]{0:T(128)S(1)} %select_n.185), channel_id=1, replica_groups=mesh['vox'=8,'fsdp'=4] {'vox','fsdp'}, use_global_device_ids=true, to_apply=%region_9.10 | all-reduce | flops 1040 | bytes 8320 | tf_op jit(solution)/shard_map/psum | solution.py:360
  (141 shorter events, 17.1 us)
Async XLA Ops:
  7.2 4.2 %copy-start = (bf16[256,1024]{1,0:T(8,128)(2,1)S(1)}, bf16[256,1024]{1,0:T(8,128)(2,1)}, u32[]{:S(2)}) copy-start(bf16[256,1024]{1,0:T(8,128)(2,1)} %param.12) | copy-start | bytes 1572868
  7.2 49.8 %all-gather.4.cloned.1.call-start = ((), (), s32[]{:S(2)}) async-start(), calls=%async_computation.4 | async-start | bytes 3932160 | tf_op jit(solution)/shard_map/all_gather | solution.py:276
  7.3 3.5 %copy-start.35 = (s32[1,6]{1,0:T(1,128)S(1)}, s32[1,6]{1,0:T(1,128)}, u32[]{:S(2)}) copy-start(s32[1,6]{1,0:T(1,128)} %param.15) | copy-start | bytes 76
  10.1 75.4 %all-gather.6.cloned.1.call-start = ((), (), s32[]{:S(2)}) async-start(), calls=%async_computation.8 | async-start | bytes 1310720 | tf_op jit(solution)/shard_map/all_gather | solution.py:277
  10.1 3.3 %collective-permute-start.1 = (bf16[384,1024]{1,0:T(8,128)(2,1)S(1)}, bf16[384,1024]{1,0:T(8,128)(2,1)}, u32[]{:S(2)}, u32[]{:S(2)}) collective-permute-start(bf16[384,1024]{1,0:T(8,128)(2,1)S(1)} %bitcast.78), channel_id=1, source_target_pairs={{0,4},{4,0},{8,12},{12,8},{16,20},{20,16},{24,28},{28,24},{1,5},{5... | collective-permute-start | bytes 2359304 | tf_op jit(solution)/shard_map/ppermute | solution.py:279
  10.6 58.4 %collective-permute-start.4 = (bf16[384,1024]{1,0:T(8,128)(2,1)}, bf16[384,1024]{1,0:T(8,128)(2,1)}, u32[]{:S(2)}, u32[]{:S(2)}) collective-permute-start(bf16[384,1024]{1,0:T(8,128)(2,1)} %bitcast.82), channel_id=1, source_target_pairs={{0,4},{4,0},{8,12},{12,8},{16,20},{20,16},{24,28},{28,24},{1,5},{5... | collective-permute-start | bytes 2359304 | tf_op jit(solution)/shard_map/ppermute | solution.py:280
  10.8 2.3 collective-permute-start
  12.1 153.2 %reduce-scatter.9.cloned.1.call-start = ((), (), s32[]{:S(2)}) async-start(), calls=%async_computation.6 | async-start | bytes 1310720 | tf_op jit(solution)/shard_map/reduce_scatter | solution.py:362
  13.4 43.6 %copy-start.33 = (f32[1024]{0:T(1024)S(1)}, f32[1024]{0:T(1024)}, u32[]{:S(2)}) copy-start(f32[1024]{0:T(1024)} %param.10) | copy-start | bytes 12292
  14.7 47.2 %copy-start.17 = (bf16[384,1024]{1,0:T(8,128)(2,1)}, bf16[384,1024]{1,0:T(8,128)(2,1)S(1)}, u32[]{:S(2)}) copy-start(bf16[384,1024]{1,0:T(8,128)(2,1)S(1)} %get-tuple-element.59) | copy-start | bytes 2359300
  15.5 53.5 %copy-start.15 = (bf16[1,384,1024]{2,1,0:T(8,128)(2,1)S(1)}, bf16[1,384,1024]{2,1,0:T(8,128)(2,1)}, u32[]{:S(2)}) copy-start(bf16[1,384,1024]{2,1,0:T(8,128)(2,1)} %param.17) | copy-start | bytes 2359300
  64.1 24.0 %collective-permute-start.2 = (bf16[192,1024]{1,0:T(8,128)(2,1)}, bf16[192,1024]{1,0:T(8,128)(2,1)S(1)}, u32[]{:S(2)}, u32[]{:S(2)}) collective-permute-start(bf16[192,1024]{1,0:T(8,128)(2,1)} %get-tuple-element.50), channel_id=1, source_target_pairs={{0,8},{4,12},{8,16},{12,20},{16,24},{20,28},{1,9},{5,13},{9,17},{1... | collective-permute-start | bytes 1179656 | tf_op jit(solution)/shard_map/ppermute | solution.py:309
  67.5 20.6 %collective-permute-start.3 = (bf16[192,1024]{1,0:T(8,128)(2,1)S(1)}, bf16[192,1024]{1,0:T(8,128)(2,1)S(1)}, u32[]{:S(2)}, u32[]{:S(2)}) collective-permute-start(bf16[192,1024]{1,0:T(8,128)(2,1)S(1)} %get-tuple-element.49), channel_id=1, source_target_pairs={{8,0},{12,4},{16,8},{20,12},{24,16},{28,20},{9,1},{13,5},{17,9},{2... | collective-permute-start | bytes 1179656 | tf_op jit(solution)/shard_map/ppermute | solution.py:310
  71.2 17.0 %copy-start.23 = (bf16[384,1024]{1,0:T(8,128)(2,1)}, bf16[384,1024]{1,0:T(8,128)(2,1)S(1)}, u32[]{:S(2)}) copy-start(bf16[384,1024]{1,0:T(8,128)(2,1)S(1)} %get-tuple-element.57) | copy-start | bytes 2359300
  85.5 38.7 %copy-start.25 = (bf16[384,1024]{1,0:T(8,128)(2,1)S(1)}, bf16[384,1024]{1,0:T(8,128)(2,1)}, u32[]{:S(2)}) copy-start(bf16[384,1024]{1,0:T(8,128)(2,1)} %get-tuple-element.58) | copy-start | bytes 2359300
  89.9 34.3 %copy-start.24 = (bf16[384,1024]{1,0:T(8,128)(2,1)S(1)}, bf16[384,1024]{1,0:T(8,128)(2,1)}, u32[]{:S(2)}) copy-start(bf16[384,1024]{1,0:T(8,128)(2,1)} %copy-done.23) | copy-start | bytes 2359300
  126.3 75.0 %reduce-scatter.7.cloned.1.call-start = ((), (), s32[]{:S(2)}) async-start(), calls=%async_computation.5 | async-start | bytes 3932160 | tf_op jit(solution)/shard_map/reduce_scatter | solution.py:368
  126.3 20.5 %collective-permute-start.6 = (f32[2,192,512]{2,1,0:T(8,128)}, f32[2,192,512]{2,1,0:T(8,128)S(1)}, u32[]{:S(2)}, u32[]{:S(2)}) collective-permute-start(f32[2,192,512]{2,1,0:T(8,128)} %copy-done.5), channel_id=1, source_target_pairs={{0,8},{4,12},{8,16},{12,20},{16,24},{20,28},{1,9},{5,13},{9,17},{1... | collective-permute-start | bytes 2359304 | tf_op jit(solution)/shard_map/ppermute | solution.py:317
  129.8 21.1 %collective-permute-start.7 = (f32[2,192,512]{2,1,0:T(8,128)}, f32[2,192,512]{2,1,0:T(8,128)S(1)}, u32[]{:S(2)}, u32[]{:S(2)}) collective-permute-start(f32[2,192,512]{2,1,0:T(8,128)} %copy-done.4), channel_id=1, source_target_pairs={{8,0},{12,4},{16,8},{20,12},{24,16},{28,20},{9,1},{13,5},{17,9},{2... | collective-permute-start | bytes 2359304 | tf_op jit(solution)/shard_map/ppermute | solution.py:316
  132.3 20.8 %copy-start.9 = (bf16[768,512]{1,0:T(8,128)(2,1)S(1)}, bf16[768,512]{1,0:T(8,128)(2,1)}, u32[]{:S(2)}) copy-start(bf16[768,512]{1,0:T(8,128)(2,1)} %copy-done.8) | copy-start | bytes 2359300
  132.3 20.8 %copy-start.18 = (bf16[384,1024]{1,0:T(8,128)(2,1)S(1)}, bf16[384,1024]{1,0:T(8,128)(2,1)}, u32[]{:S(2)}) copy-start(bf16[384,1024]{1,0:T(8,128)(2,1)} %copy-done.17) | copy-start | bytes 2359300
  132.3 20.8 %copy-start.20 = (bf16[384,1024]{1,0:T(8,128)(2,1)S(1)}, bf16[384,1024]{1,0:T(8,128)(2,1)}, u32[]{:S(2)}) copy-start(bf16[384,1024]{1,0:T(8,128)(2,1)} %copy-done.19) | copy-start | bytes 2359300
  132.3 19.9 %copy-start.26 = (bf16[384,512]{1,0:T(8,128)(2,1)}, bf16[384,512]{1,0:T(8,128)(2,1)S(1)}, u32[]{:S(2)}) copy-start(bf16[384,512]{1,0:T(8,128)(2,1)S(1)} %slice.112) | copy-start | bytes 1179652
  157.7 65.5 %reduce-scatter.11.cloned.1.call-start = ((), (), s32[]{:S(2)}) async-start(), calls=%async_computation.7 | async-start | bytes 327680 | tf_op jit(solution)/shard_map/reduce_scatter | solution.py:365
  165.3 82.1 %reduce-scatter.13.cloned.1.call-start = ((), (), s32[]{:S(2)}) async-start(), calls=%async_computation.9 | async-start | bytes 983040
  168.2 35.3 %copy-start.21 = (bf16[1,1,512,1024]{3,2,1,0:T(8,128)(2,1)S(1)}, bf16[1,1,512,1024]{3,2,1,0:T(8,128)(2,1)}, u32[]{:S(2)}) copy-start(bf16[1,1,512,1024]{3,2,1,0:T(8,128)(2,1)} %all-gather.6.cloned.1.call-done) | copy-start | bytes 3145732
  168.2 39.6 %collective-permute-start.8 = (f32[384,1024]{1,0:T(8,128)}, f32[384,1024]{1,0:T(8,128)}, u32[]{:S(2)}, u32[]{:S(2)}) collective-permute-start(f32[384,1024]{1,0:T(8,128)} %constant_dynamic-slice_fusion.2), channel_id=1, source_target_pairs={{0,4},{4,0},{8,12},{12,8},{16,20},{20,16},{24,28},{28,24},{1,5},{5... | collective-permute-start | bytes 4718600 | tf_op jit(solution)/shard_map/ppermute | solution.py:342
  207.4 41.0 %collective-permute-start.5 = (f32[384,1024]{1,0:T(8,128)}, f32[384,1024]{1,0:T(8,128)}, u32[]{:S(2)}, u32[]{:S(2)}) collective-permute-start(f32[384,1024]{1,0:T(8,128)} %constant_dynamic-slice_fusion.3), channel_id=1, source_target_pairs={{0,4},{4,0},{8,12},{12,8},{16,20},{20,16},{24,28},{28,24},{1,5},{5... | collective-permute-start | bytes 4718600 | tf_op jit(solution)/shard_map/ppermute | solution.py:324
  207.8 40.7 %copy-start.16 = (bf16[1,384,1024]{2,1,0:T(8,128)(2,1)S(1)}, bf16[1,384,1024]{2,1,0:T(8,128)(2,1)}, u32[]{:S(2)}) copy-start(bf16[1,384,1024]{2,1,0:T(8,128)(2,1)} %param.17) | copy-start | bytes 2359300
  224.0 67.4 %collective-permute-start.10 = (f32[128,128]{1,0:T(8,128)S(1)}, f32[128,128]{1,0:T(8,128)S(1)}, u32[]{:S(2)}, u32[]{:S(2)}) collective-permute-start(f32[128,128]{1,0:T(8,128)S(1)} %constant_dynamic-slice_fusion), channel_id=1, source_target_pairs={{0,4},{4,0},{8,12},{12,8},{16,20},{20,16},{24,28},{28,24},{1,5},{5... | collective-permute-start | bytes 196616 | tf_op jit(solution)/shard_map/ppermute | solution.py:377
  248.4 43.8 %collective-permute-start.9 = (f32[256,384]{0,1:T(8,128)S(1)}, f32[256,384]{0,1:T(8,128)S(1)}, u32[]{:S(2)}, u32[]{:S(2)}) collective-permute-start(f32[256,384]{0,1:T(8,128)S(1)} %bitcast_convert_fusion), channel_id=1, source_target_pairs={{0,4},{4,0},{8,12},{12,8},{16,20},{20,16},{24,28},{28,24},{1,5},{5... | collective-permute-start | bytes 1179656 | tf_op jit(solution)/shard_map/ppermute | solution.py:390
  248.4 43.7 %copy-start.22 = (bf16[384,256]{1,0:T(8,128)(2,1)S(1)}, bf16[384,256]{1,0:T(8,128)(2,1)}, u32[]{:S(2)}) copy-start(bf16[384,256]{1,0:T(8,128)(2,1)} %reduce-scatter.13.cloned.1.call-done) | copy-start | bytes 589828
  (22 other events, 35.7 us)
Sparse Core Ops, SparseCore 0:
  10.4 46.5 all-gather.3
  58.8 26.6 all-gather.5
  126.4 27.6 reduce-scatter.8
  157.8 43.3 reduce-scatter.6
  203.4 19.6 reduce-scatter.10
  225.9 21.4 reduce-scatter.12

commit v2 on v1

--- a/solution.py
+++ b/solution.py
@@ -151,27 +151,28 @@
         grad_k = unit_back(k_unit[place, :], k_len[place, :], dk[place, :], same_head)
         grad_v = dv[place, :]
         if part < margin:
-            rim_b_ref[0, place, :] = grad_k
-            rim_b_ref[1, place, :] = grad_v
+            rim_b_ref[0, place, :] = grad_k.astype(BF)
+            rim_b_ref[1, place, :] = grad_v.astype(BF)
         elif part < margin + rows:
             here = slice(part - margin, part - margin + 64)
             dk_ref[here, :] = grad_k
             dv_ref[here, :] = grad_v
         else:
             here = slice(part - margin - rows, part - margin - rows + 64)
-            rim_a_ref[0, here, :] = grad_k
-            rim_a_ref[1, here, :] = grad_v
+            rim_a_ref[0, here, :] = grad_k.astype(BF)
+            rim_a_ref[1, here, :] = grad_v.astype(BF)
     ds_ref[0, :, :] = ds
 
 
-def attention(packed, before, after, upstream, mult, valid, scales):
+def attention(packed, before, after, upstream, mult, valid, scales, pairs):
     rows, width3 = packed.shape
     width = width3 // 3
     margin = before.shape[0]
     pool = rows + 2 * margin
-    pairs = width // PAIR
+    count = len(pairs)
     steps = rows // PAIR
     span = WINDOW * BLK
+    first, stride = pairs[0], pairs[1] - pairs[0]
 
     def at(offset):
         return lambda p, *_: (0, offset + p)
@@ -180,16 +181,16 @@
         attention_kernel,
         grid_spec=pltpu.PrefetchScalarGridSpec(
             num_scalar_prefetch=3,
-            grid=(pairs,),
+            grid=(count,),
             in_specs=[
                 pl.BlockSpec((rows, PAIR), at(0)),
-                pl.BlockSpec((rows, PAIR), at(pairs)),
-                pl.BlockSpec((rows, PAIR), at(2 * pairs)),
+                pl.BlockSpec((rows, PAIR), at(count)),
+                pl.BlockSpec((rows, PAIR), at(2 * count)),
                 pl.BlockSpec((margin, PAIR), at(0)),
-                pl.BlockSpec((margin, PAIR), at(pairs)),
+                pl.BlockSpec((margin, PAIR), at(count)),
                 pl.BlockSpec((margin, PAIR), at(0)),
-                pl.BlockSpec((margin, PAIR), at(pairs)),
-                pl.BlockSpec((rows, PAIR), at(0)),
+                pl.BlockSpec((margin, PAIR), at(count)),
+                pl.BlockSpec((rows, PAIR), lambda p, *_: (0, first + stride * p)),
             ],
             out_specs=[
                 pl.BlockSpec((rows, PAIR), at(0)),
@@ -222,31 +223,97 @@
             jax.ShapeDtypeStruct((rows, width), BF),
             jax.ShapeDtypeStruct((rows, width), F32),
             jax.ShapeDtypeStruct((rows, width), F32),
-            jax.ShapeDtypeStruct((2, margin, width), F32),
-            jax.ShapeDtypeStruct((2, margin, width), F32),
-            jax.ShapeDtypeStruct((pairs, 8, 2 * PAIR), F32),
+            jax.ShapeDtypeStruct((2, margin, width), BF),
+            jax.ShapeDtypeStruct((2, margin, width), BF),
+            jax.ShapeDtypeStruct((count, 8, 2 * PAIR), F32),
         ],
         compiler_params=pltpu.CompilerParams(vmem_limit_bytes=40 * 1024 * 1024),
         cost_estimate=pl.CostEstimate(
-            flops=2 * 6 * pairs * steps * span * 256 * 128,
+            flops=8 * 2 * 6 * count * steps * span * 256 * 128,
             bytes_accessed=packed.size * 2 + rows * width * 14,
-            transcendentals=pairs * steps * span * 256,
+            transcendentals=count * steps * span * 256,
         ),
         name="block_attention",
     )(mult, valid, scales, packed, packed, packed, before, before, after, after, upstream)
 
 
 def pick_groups(array, axis, unit, core):
-    shape = array.shape
-    split = shape[:axis] + (shape[axis] // (2 * unit), 2, unit) + shape[axis + 1 :]
-    picked = lax.dynamic_index_in_dim(array.reshape(split), core, axis + 1, keepdims=False)
-    return picked.reshape(shape[:axis] + (shape[axis] // 2,) + shape[axis + 1 :])
+    size = array.shape[axis]
+    picked = [
+        jnp.where(
+            core == 0,
+            lax.slice_in_dim(array, at, at + unit, axis=axis),
+            lax.slice_in_dim(array, at + unit, at + 2 * unit, axis=axis),
+        )
+        for at in range(0, size, 2 * unit)
+    ]
+    return jnp.concatenate(picked, axis=axis)
+
+
+def spread_groups(array, axis, unit, core):
+    groups = jnp.split(array, array.shape[axis] // unit, axis=axis)
+    parts = []
+    for group in groups:
+        empty = jnp.zeros_like(group)
+        parts += [jnp.where(core == 0, group, empty), jnp.where(core == 0, empty, group)]
+    return jnp.concatenate(parts, axis=axis)
 
 
 def in_order(core, own, other, axis):
     first = jnp.where(core == 0, own, other)
     second = jnp.where(core == 0, other, own)
     return jnp.concatenate([first, second], axis=axis)
+
+
+def xor_blocks(blocks, index):
+    odd = (index & 1) == 1
+    high = (index & 2) == 2
+    near = [jnp.where(odd, blocks[k ^ 1], blocks[k]) for k in range(4)]
+    return [jnp.where(high, near[k ^ 2], near[k]) for k in range(4)]
+
+
+ORDER = (1, 3, 2, 0)
+CHUNKS = ((0, 3), (1, 2))
+
+
+def square(value, step):
+    return lax.ppermute(value, "fsdp", [(i, i ^ step) for i in range(4)])
+
+
+def gather_square(shard):
+    half = shard.shape[0] // 2
+    near = square(shard, 1)
+    far = square(shard, 2)
+    top = square(far[:half], 1)
+    low = square(near[half:], 2)
+    return [near, jnp.concatenate([top, low], axis=0), far, shard]
+
+
+def chips(value, step, n_vox):
+    return lax.ppermute(value, "vox", [(i, i ^ (2 * step)) for i in range(n_vox)])
+
+
+def reduce_square(normed_blocks, grad):
+    half = grad.shape[1] // 2
+    one, three, two, zero = normed_blocks
+    left, right = grad[:, :half], grad[:, half:]
+    t = ((0,), (0,))
+
+    def both(a, b):
+        return jnp.concatenate([a, b], axis=1)
+
+    got_left = square(dot(both(one, three), left, t).astype(BF), 1)
+    got_right = square(dot(both(three, two), right, t).astype(BF), 2)
+    size = zero.shape[1]
+    pass_left = dot(two, left, t) + got_left[size:].astype(F32)
+    pass_right = dot(one, right, t) + got_right[:size].astype(F32)
+    end_left = square(pass_left.astype(BF), 2)
+    end_right = square(pass_right.astype(BF), 1)
+    kept_left = dot(zero, left, t) + got_left[:size].astype(F32)
+    kept_right = dot(zero, right, t) + got_right[size:].astype(F32)
+    return jnp.concatenate(
+        [kept_left + end_left.astype(F32), kept_right + end_right.astype(F32)], axis=1
+    )
 
 
 def on_device(
@@ -262,19 +329,43 @@
     reach = own_blocks // 2
     margin = reach * BLK
     n_vox = lax.axis_size("vox")
+    n_fsdp = lax.axis_size("fsdp")
     n_chip = n_vox // 2
     place = lax.axis_index("vox")
+    scene = lax.axis_index("fsdp")
     core = place % 2
     chip = place // 2
-    chip_columns = 3 * model_width // n_chip
-    unit = 128 if chip_columns % 256 == 0 and w_out.shape[0] % 256 == 0 else 64
+    fast = n_vox == 8 and n_fsdp == 4
+    unit = 128 if fast else 64
     swap = [(i, i ^ 1) for i in range(n_vox)]
     up = [(i, i + 2) for i in range(n_vox - 2)]
     down = [(j, i) for i, j in up]
-    same_core = [[2 * i + c for i in range(n_chip)] for c in range(2)]
-
-    qkv_half = lax.all_gather(pick_groups(w_qkv, 1, unit, core), "fsdp", axis=0, tiled=True)
-    out_half = lax.all_gather(pick_groups(w_out, 0, unit, core), "fsdp", axis=0, tiled=True)
+    part_width = model_width // 2
+
+    def columns_of(array, pairs):
+        return jnp.concatenate(
+            [
+                array[:, base + p * PAIR : base + (p + 1) * PAIR]
+                for base in range(0, array.shape[1], part_width)
+                for p in pairs
+            ],
+            axis=1,
+        )
+
+    core_qkv = pick_groups(w_qkv, 1, unit, core)
+    core_out = pick_groups(w_out, 0, unit, core)
+    if fast:
+        qkv_chunks = [
+            jnp.concatenate(gather_square(columns_of(core_qkv, pairs)), axis=0) for pairs in CHUNKS
+        ]
+        one, three, two, zero = gather_square(core_out)
+        out_half = jnp.concatenate(xor_blocks([zero, one, two, three], scene), axis=0)
+    else:
+        qkv_chunks = [
+            lax.all_gather(columns_of(core_qkv, pairs), "fsdp", axis=0, tiled=True)
+            for pairs in CHUNKS
+        ]
+        out_half = lax.all_gather(core_out, "fsdp", axis=0, tiled=True)
 
     other_tokens = lax.ppermute(own_tokens, "vox", swap)
     other_cotangent = lax.ppermute(own_cotangent, "vox", swap)
@@ -299,47 +390,96 @@
     scene_total = valid_voxels.shape[1]
     pool_ids = first_block - reach + jnp.arange(pool_blocks, dtype=jnp.int32)
     valid = jnp.take(valid_voxels[0], jnp.clip(pool_ids, 0, scene_total - 1))
-    scales = pick_groups(logit_scale, 0, unit // HD, core)
+    group_heads = unit // HD
+    scales = pick_groups(logit_scale, 0, group_heads, core)
 
     wide = chip_tokens.astype(F32)
     inverse = lax.rsqrt(jnp.mean(wide * wide, axis=1, keepdims=True) + EPS)
     normed = (wide * inverse * gain).astype(BF)
-    packed = dot(normed, qkv_half).astype(BF)
-    width = packed.shape[1] // 3
-    before = lax.ppermute(packed[rows - margin :, width:], "vox", up)
-    after = lax.ppermute(packed[:margin, width:], "vox", down)
+    if fast:
+        turned = xor_blocks(jnp.split(normed, 4, axis=1), scene)
+        normed_blocks = [turned[k] for k in ORDER]
+        normed = jnp.concatenate(normed_blocks, axis=1)
+
+    packed_chunks, halos = [], []
+    for weight in qkv_chunks:
+        packed = dot(normed, weight).astype(BF)
+        width = packed.shape[1] // 3
+        before = lax.ppermute(packed[rows - margin :, width:], "vox", up)
+        after = lax.ppermute(packed[:margin, width:], "vox", down)
+        packed_chunks.append(packed)
+        halos.append((before, after))
     upstream = dot(chip_cotangent, out_half, ((1,), (1,))).astype(BF)
 
-    att, dq, dk, dv, rim_b, rim_a, ds = attention(
-        packed, before, after, upstream, mult, valid, scales
-    )
-    back_a = lax.ppermute(rim_b, "vox", down)
-    back_b = lax.ppermute(rim_a, "vox", up)
-
-    out_grad = dot(att, chip_cotangent, ((0,), (0,)))
-    mixed_part = dot(att, out_half)
+    mixed_part = 0.0
+    ngrad_part = 0.0
+    scale_parts = {}
+    qkv_sums, out_sums = [], []
+    for chunk, pairs in enumerate(CHUNKS):
+        chunk_scales = jnp.concatenate([scales[2 * p : 2 * p + 2] for p in pairs])
+        att, dq, dk, dv, rim_b, rim_a, ds = attention(
+            packed_chunks[chunk], *halos[chunk], upstream, mult, valid, chunk_scales, pairs
+        )
+        back_a = lax.ppermute(rim_b, "vox", down).astype(F32)
+        back_b = lax.ppermute(rim_a, "vox", up).astype(F32)
+        head_sums_of = jnp.sum(ds.reshape(-1, 8, 2, PAIR), axis=(1, 3))
+        for i, p in enumerate(pairs):
+            scale_parts[p] = head_sums_of[i]
+
+        out_rows = jnp.concatenate([out_half[p * PAIR : (p + 1) * PAIR] for p in pairs], axis=0)
+        mixed_part = mixed_part + dot(att, out_rows)
+        out_grad = dot(att, chip_cotangent, ((0,), (0,)))
+
+        def with_rims(grad, index):
+            return jnp.concatenate(
+                [
+                    grad[:margin] + back_b[index],
+                    grad[margin : rows - margin],
+                    grad[rows - margin :] + back_a[index],
+                ],
+                axis=0,
+            ).astype(BF)
+
+        grad_packed = jnp.concatenate([dq, with_rims(dk, 0), with_rims(dv, 1)], axis=1)
+        ngrad_part = ngrad_part + dot(grad_packed, qkv_chunks[chunk], ((1,), (1,)))
+        if fast:
+            even, low = chip % 2 == 0, chip < 2
+            quarter = model_width // 4
+            cols = [out_grad[:, k * quarter : (k + 1) * quarter] for k in range(4)]
+            kept = [jnp.where(even, cols[k], cols[k + 1]) for k in (0, 2)]
+            sent = [jnp.where(even, cols[k + 1], cols[k]) for k in (0, 2)]
+            got = chips(jnp.concatenate(sent, axis=1).astype(BF), 1, n_vox).astype(F32)
+            kept = [kept[0] + got[:, :quarter], kept[1] + got[:, quarter:]]
+            got = chips(jnp.where(low, kept[1], kept[0]).astype(BF), 2, n_vox).astype(F32)
+            out_sums.append(jnp.where(low, kept[0], kept[1]) + got)
+
+            part = reduce_square(normed_blocks, grad_packed)
+            groups = [part[:, k * PAIR : (k + 1) * PAIR] for k in range(6)]
+            sets = ((0, 3, 4), (1, 2, 5)) if chunk == 0 else ((0, 1, 3), (2, 4, 5))
+            evens, odds = [jnp.concatenate([groups[k] for k in s], axis=1) for s in sets]
+            got = chips(jnp.where(even, odds, evens).astype(BF), 1, n_vox).astype(F32)
+            kept = jnp.where(even, evens, odds) + got
+            left, right = kept[:, : 2 * PAIR], kept[:, PAIR:]
+            got = chips(jnp.where(low, right, left).astype(BF), 2, n_vox).astype(F32)
+            qkv_sums.append(jnp.where(low, left, right) + got)
+        else:
+            out_sums.append(out_grad)
+            qkv_sums.append(dot(normed, grad_packed, ((0,), (0,))))
+
     mixed_mine = lax.dynamic_slice_in_dim(mixed_part, core * own_rows, own_rows, 0)
     mixed_theirs = lax.dynamic_slice_in_dim(mixed_part, (1 - core) * own_rows, own_rows, 0)
     mixed = (
         own_tokens.astype(F32) + (mixed_mine + lax.ppermute(mixed_theirs, "vox", swap))
     ).astype(BF)
 
-    def with_rims(grad, index):
-        return jnp.concatenate(
-            [
-                grad[:margin] + back_b[index],
-                grad[margin : rows - margin],
-                grad[rows - margin :] + back_a[index],
-            ],
-            axis=0,
-        ).astype(BF)
-
-    grad_packed = jnp.concatenate([dq, with_rims(dk, 0), with_rims(dv, 1)], axis=1)
-    qkv_grad = dot(normed, grad_packed, ((0,), (0,)))
-    ngrad_part = dot(grad_packed, qkv_half, ((1,), (1,)))
     ngrad_mine = lax.dynamic_slice_in_dim(ngrad_part, core * own_rows, own_rows, 0)
     ngrad_theirs = lax.dynamic_slice_in_dim(ngrad_part, (1 - core) * own_rows, own_rows, 0)
     normed_grad = ngrad_mine + lax.ppermute(ngrad_theirs, "vox", swap)
+    if fast:
+        held = jnp.split(normed_grad, 4, axis=1)
+        normed_grad = jnp.concatenate(
+            xor_blocks([held[ORDER.index(k)] for k in range(4)], scene), axis=1
+        )
 
     own_wide = own_tokens.astype(F32)
     own_inverse = lax.rsqrt(jnp.mean(own_wide * own_wide, axis=1, keepdims=True) + EPS)
@@ -353,48 +493,71 @@
         * jnp.mean(scaled_grad * own_wide, axis=1, keepdims=True)
     )
 
-    group_heads = unit // HD
-    scale_part = jnp.sum(ds.reshape(-1, 8, 2, PAIR), axis=(1, 3)).reshape(-1, 1, group_heads)
-    mine = (jnp.arange(2) == core)[None, :, None]
-    scale_grad = jnp.where(mine, scale_part, 0.0).reshape(HEADS)
-    summed_gain, summed_scale = lax.psum((gain_grad, scale_grad), ("vox", "fsdp"))
-
-    out_part = lax.psum_scatter(
-        out_grad.astype(BF), "fsdp", scatter_dimension=0, tiled=True
-    )
-    out_sum = lax.psum_scatter(
-        out_part, "vox", scatter_dimension=1, tiled=True, axis_index_groups=same_core
-    ).astype(F32)
-    qkv_part = lax.psum_scatter(
-        qkv_grad.astype(BF), "fsdp", scatter_dimension=0, tiled=True
-    )
-    qkv_sum = lax.psum_scatter(
-        qkv_part, "vox", scatter_dimension=1, tiled=True, axis_index_groups=same_core
-    ).astype(F32)
-
-    half = out_sum.shape[1] // 2
-    out_mine = lax.dynamic_slice_in_dim(out_sum, core * half, half, 1)
-    out_theirs = lax.ppermute(
-        lax.dynamic_slice_in_dim(out_sum, (1 - core) * half, half, 1), "vox", swap
-    )
-    sets = out_sum.shape[0] // unit
-    out_both = in_order(
-        core,
-        out_mine.reshape(sets, 1, unit, half),
-        out_theirs.reshape(sets, 1, unit, half),
-        1,
-    )
-    summed_out = out_both.reshape(2 * sets * unit, half)
-
-    height, held = qkv_sum.shape
-    qkv_other = lax.ppermute(qkv_sum, "vox", swap)
-    qkv_both = in_order(
-        core,
-        qkv_sum.reshape(height, held // unit, 1, unit),
-        qkv_other.reshape(height, held // unit, 1, unit),
-        2,
-    ).reshape(height, 2 * held)
-    summed_qkv = lax.dynamic_slice_in_dim(qkv_both, core * held, held, 1)
+    scale_part = jnp.concatenate([scale_parts[p] for p in range(len(scale_parts))])
+    scale_grad = spread_groups(scale_part, 0, group_heads, core)
+    if fast:
+        small = jnp.concatenate([gain_grad, scale_grad, jnp.zeros((112,), F32)]).reshape(9, 128)
+        for step in (1, 2):
+            small = small + square(small, step)
+        for step in (1, 2, 4):
+            small = small + lax.ppermute(small, "vox", [(i, i ^ step) for i in range(n_vox)])
+        small = small.reshape(-1)
+        summed_gain, summed_scale = small[:model_width], small[model_width : model_width + HEADS]
+    else:
+        summed_gain, summed_scale = lax.psum((gain_grad, scale_grad), ("vox", "fsdp"))
+
+    if fast:
+        by_pair = {}
+        for pairs, total in zip(CHUNKS, out_sums):
+            for i, p in enumerate(pairs):
+                by_pair[p] = total[i * PAIR : (i + 1) * PAIR]
+        turned = xor_blocks([by_pair[p] for p in range(4)], scene)
+        out_sum = turned[0]
+        for step in (1, 2, 3):
+            out_sum = out_sum + square(turned[step].astype(BF), step).astype(F32)
+        half = out_sum.shape[1] // 2
+        first, second = out_sum[:, :half], out_sum[:, half:]
+        out_other = lax.ppermute(jnp.where(core == 0, second, first), "vox", swap)
+        summed_out = in_order(core, jnp.where(core == 0, first, second), out_other, 0)
+
+        a0, a1 = qkv_sums[0][:, :PAIR], qkv_sums[0][:, PAIR:]
+        b0, b1 = qkv_sums[1][:, :PAIR], qkv_sums[1][:, PAIR:]
+
+        def by_chip(options):
+            value = options[3]
+            for k in range(3):
+                value = jnp.where(chip == k, options[k], value)
+            return value
+
+        g0 = by_chip((a0, a0, b1, b0))
+        g1 = by_chip((b0, a1, a0, b1))
+        g2 = by_chip((b1, b0, a1, a1))
+        got = lax.ppermute(jnp.where(core == 0, g2, g0), "vox", swap)
+        summed_qkv = jnp.concatenate(
+            [
+                jnp.where(core == 0, g0, g1),
+                got,
+                jnp.where(core == 0, g1, g2),
+            ],
+            axis=1,
+        )
+    else:
+        by_pair = {}
+        cols = {}
+        for pairs, out_total, qkv_total in zip(CHUNKS, out_sums, qkv_sums):
+            for i, p in enumerate(pairs):
+                by_pair[p] = out_total[i * PAIR : (i + 1) * PAIR]
+                for j in range(3):
+                    at = (2 * j + i) * PAIR
+                    cols[4 * j + p] = qkv_total[:, at : at + PAIR]
+        out_total = jnp.concatenate([by_pair[p] for p in range(4)], axis=0)
+        qkv_total = jnp.concatenate([cols[k] for k in range(12)], axis=1)
+        out_total = spread_groups(out_total, 0, unit, core)
+        qkv_total = lax.psum_scatter(qkv_total, "fsdp", scatter_dimension=0, tiled=True)
+        qkv_total = spread_groups(qkv_total, 1, unit, core)
+        summed_qkv = lax.psum_scatter(qkv_total, "vox", scatter_dimension=1, tiled=True)
+        out_total = lax.psum_scatter(out_total, "fsdp", scatter_dimension=0, tiled=True)
+        summed_out = lax.psum_scatter(out_total, "vox", scatter_dimension=1, tiled=True)
 
     return (
         mixed[None],

time: 301 us -> 246 us (0.82)
  waiting for transfers between devices: 142 us -> 80.6 us
  starting transfers between devices: 11.3 us -> 62.8 us
  blocking collectives: 38.7 us -> 0 us
  other arithmetic: 16.3 us -> 30.8 us
  between operations: 14.6 us -> 2.14 us
  local copies, waits for them, and re-layouts: 25.2 us -> 17.5 us
    ppermute x4 -> x42, waiting for transfers between devices: 18.5 us -> 78.8 us  [the longest x25 51.9 us: square(): return lax.ppermute(value, 'fsdp', [(i, i ^ step) for i in range(4)])]
    all_gather x2 -> x0, waiting for transfers between devices: 55.8 us -> none  [the longest x1 41.4 us: on_device(): lax.all_gather(pick_groups(w_qkv, 1, unit, core), 'fsdp', axis=0, tiled=T...]
    ppermute x4 -> x42, starting transfers between devices: 4.89 us -> 50.2 us  [the longest x25 24.7 us: square(): return lax.ppermute(value, 'fsdp', [(i, i ^ step) for i in range(4)])]
    reduce_scatter x3 -> x0, waiting for transfers between devices: 44.4 us -> none  [the longest x1 32.8 us: on_device(): lax.psum_scatter(qkv_grad.astype(BF), 'fsdp', scatter_dimension=0, tiled=...]
    psum x1 -> x0, blocking collectives: 38.7 us -> none  [on_device(): lax.psum((gain_grad, scale_grad), ('vox', 'fsdp'))]
    unnamed x7 -> x0, waiting for transfers between devices: 23.4 us -> none
    unnamed x0 -> x13, other arithmetic: none -> 9.03 us
    unnamed x77 -> x135, local copies, waits for them, and re-layouts: 16 us -> 10 us
  transfers between devices with their start and end apart: 17 -> 51, of which waited for: 7 -> 25; matrix products, arithmetic and copies ran while one was open for 15% -> 21% of each run, Pallas kernels for 0% -> 13%
where the time goes in v2:
time: 246 us; the launch traced here: 245 us
  waiting for transfers between devices  80.6 us (33%)
  starting transfers between devices  62.8 us (26%)
  Pallas kernels  31.6 us (13%)
  other arithmetic  30.8 us (13%)
  matrix products  19.8 us (8%)
  local copies, waits for them, and re-layouts  17.5 us (7%)
    ppermute x25, waiting for transfers between devices, square(): return lax.ppermute(value, 'fsdp', [(i, i ^ step) for i in range(4)])  51.9 us
    pallas_call x2, Pallas kernels, attention(): pl.pallas_call(attention_kernel, grid_spec=pltpu.PrefetchScalarGridSpec(n...  31.6 us
    ppermute x25, starting transfers between devices, square(): return lax.ppermute(value, 'fsdp', [(i, i ^ step) for i in range(4)])  24.7 us
    ppermute x8, waiting for transfers between devices, chips(): return lax.ppermute(value, 'vox', [(i, i ^ 2 * step) for i in range(n_vox)])  21 us
    dot_general x21, matrix products, dot(): return lax.dot_general(a, b, (dims, ((), ())), preferred_element_type=F32)  19.8 us
    ppermute x8, starting transfers between devices, chips(): return lax.ppermute(value, 'vox', [(i, i ^ 2 * step) for i in range(n_vox)])  11.3 us
    unnamed x135, local copies, waits for them, and re-layouts  10 us
    ppermute x2, starting transfers between devices, on_device(): back_b = lax.ppermute(rim_a, 'vox', up).astype(F32)  9.74 us
  transfers between devices with their start and end apart: 51, of which 25 were waited for; matrix products, arithmetic and copies ran while one was open for 21% of the time, Pallas kernels for 13%

profile of v2, /device:TPU:0, one launch (start us, length us, event | category | flops | bytes accessed | tf_op | source)
XLA Modules:
  0.0 245.1 jit_solution(1122415801059047559)
XLA Ops:
  2.6 2.9 %collective-permute-start.11 = (bf16[128,1024]{1,0:T(8,128)(2,1)}, bf16[128,1024]{1,0:T(8,128)(2,1)S(1)}, u32[]{:S(2)}, u32[]{:S(2)}) collective-permute-start(bf16[128,1024]{1,0:T(8,128)(2,1)} %slice_select_fusion.4), channel_id=1, source_target_pairs={{0,1},{1,0},{2,3},{3,2},{4,5},{5,4},{6,7},{7,6},{8,9},{9,8},{10,11... | collective-permute-start | bytes 786440 | tf_op jit(solution)/shard_map/ppermute | solution.py:280
  20.3 2.0 collective-permute-start.3
  25.4 5.3 %collective-permute-done.10 = bf16[64,1024]{1,0:T(8,128)(2,1)S(1)} collective-permute-done((bf16[64,1024]{1,0:T(8,128)(2,1)S(1)}, bf16[64,1024]{1,0:T(8,128)(2,1)S(1)}, u32[]{:S(2)}, u32[]{:S(2)}) %collective-permute-start.10) | collective-permute-done | bytes 131104 | tf_op jit(solution)/shard_map/ppermute | solution.py:280
  31.0 7.9 %collective-permute-done.12 = bf16[64,1024]{1,0:T(8,128)(2,1)S(1)} collective-permute-done((bf16[64,1024]{1,0:T(8,128)(2,1)}, bf16[64,1024]{1,0:T(8,128)(2,1)S(1)}, u32[]{:S(2)}, u32[]{:S(2)}) %collective-permute-start.12) | collective-permute-done | bytes 131104 | tf_op jit(solution)/shard_map/ppermute | solution.py:280
  43.8 8.2 %collective-permute-done.4 = bf16[128,768]{1,0:T(8,128)(2,1)S(1)} collective-permute-done((bf16[128,768]{1,0:T(8,128)(2,1)S(1)}, bf16[128,768]{1,0:T(8,128)(2,1)S(1)}, u32[]{:S(2)}, u32[]{:S(2)}) %collective-permute-start.4) | collective-permute-done | bytes 196640 | tf_op jit(solution)/shard_map/ppermute | solution.py:280
  52.6 5.3 %collective-permute-done.16 = bf16[128,768]{1,0:T(8,128)(2,1)S(1)} collective-permute-done((bf16[128,768]{1,0:T(8,128)(2,1)S(1)}, bf16[128,768]{1,0:T(8,128)(2,1)S(1)}, u32[]{:S(2)}, u32[]{:S(2)}) %collective-permute-start.16) | collective-permute-done | bytes 196640 | tf_op jit(solution)/shard_map/ppermute | solution.py:280
  63.4 4.6 %collective-permute-start.6 = (bf16[192,512]{1,0:T(8,128)(2,1)}, bf16[192,512]{1,0:T(8,128)(2,1)S(1)}, u32[]{:S(2)}, u32[]{:S(2)}) collective-permute-start(bf16[192,512]{1,0:T(8,128)(2,1)} %get-tuple-element.76), channel_id=1, source_target_pairs={{0,8},{4,12},{8,16},{12,20},{16,24},{20,28},{1,9},{5,13},{9,17},{1... | collective-permute-start | bytes 589832 | tf_op jit(solution)/shard_map/ppermute | solution.py:408
  70.8 4.7 %collective-permute-start.17 = (bf16[192,512]{1,0:T(8,128)(2,1)S(1)}, bf16[192,512]{1,0:T(8,128)(2,1)S(1)}, u32[]{:S(2)}, u32[]{:S(2)}) collective-permute-start(bf16[192,512]{1,0:T(8,128)(2,1)S(1)} %get-tuple-element.78), channel_id=1, source_target_pairs={{0,8},{4,12},{8,16},{12,20},{16,24},{20,28},{1,9},{5,13},{9,17},{1... | collective-permute-start | bytes 589832 | tf_op jit(solution)/shard_map/ppermute | solution.py:408
  78.5 16.1 %block_attention.3 = (bf16[768,256]{1,0:T(8,128)(2,1)S(1)}, bf16[768,256]{1,0:T(8,128)(2,1)S(1)}, f32[768,256]{1,0:T(8,128)S(1)}, f32[768,256]{1,0:T(8,128)S(1)}...) custom-call(s32[12,8]{1,0:T(8,128)S(1)} %copy.22.mult_ref, ...), custom_call_target="tpu_custom_call" | custom-call | flops 19327352832 | bytes 3932160 | tf_op jit(solution)/shard_map/block_attention/pallas_call | solution.py:180
  97.4 5.1 %collective-permute-start.22 = (bf16[2,192,256]{2,1,0:T(8,128)(2,1)}, bf16[2,192,256]{2,1,0:T(8,128)(2,1)}, u32[]{:S(2)}, u32[]{:S(2)}) collective-permute-start(bf16[2,192,256]{2,1,0:T(8,128)(2,1)} %get-tuple-element.29), channel_id=1, source_target_pairs={{0,8},{4,12},{8,16},{12,20},{16,24},{20,28},{1,9},{5,13},{9,17},{1... | collective-permute-start | bytes 589832 | tf_op jit(solution)/shard_map/ppermute | solution.py:424
  104.0 3.3 %fusion.56 = f32[768,1024]{1,0:T(8,128)} fusion(bf16[768,256]{1,0:T(8,128)(2,1)S(1)} %get-tuple-element.21, bf16[128,1024]{1,0:T(8,128)(2,1)} %copy-done.40, bf16[128,1024]{1,0:T(8,128)(2,1)S(1)} %get-tuple-element.84), kind=kOutput, calls=%fused_computation.102 | convolution fusion | flops 403701760 | bytes 4063232 | tf_op jit(solution)/shard_map/dot_general | solution.py:22
  112.1 15.5 %block_attention.2 = (bf16[768,256]{1,0:T(8,128)(2,1)S(1)}, bf16[768,256]{1,0:T(8,128)(2,1)S(1)}, f32[768,256]{1,0:T(8,128)S(1)}, f32[768,256]{1,0:T(8,128)S(1)}...) custom-call(s32[12,8]{1,0:T(8,128)S(1)} %copy-done.5, ...), custom_call_target="tpu_custom_call" | custom-call | flops 19327352832 | bytes 3932160 | tf_op jit(solution)/shard_map/block_attention/pallas_call | solution.py:180
  131.2 4.7 %collective-permute-start.20 = (bf16[2,192,256]{2,1,0:T(8,128)(2,1)}, bf16[2,192,256]{2,1,0:T(8,128)(2,1)S(1)}, u32[]{:S(2)}, u32[]{:S(2)}) collective-permute-start(bf16[2,192,256]{2,1,0:T(8,128)(2,1)} %copy-done.11), channel_id=1, source_target_pairs={{0,8},{4,12},{8,16},{12,20},{16,24},{20,28},{1,9},{5,13},{9,17},{1... | collective-permute-start | bytes 589832 | tf_op jit(solution)/shard_map/ppermute | solution.py:424
  137.5 2.1 fusion.61
  139.8 2.7 %collective-permute-start.38 = (bf16[256,512]{1,0:T(8,128)(2,1)S(1)}, bf16[256,512]{1,0:T(8,128)(2,1)S(1)}, u32[]{:S(2)}, u32[]{:S(2)}) collective-permute-start(bf16[256,512]{1,0:T(8,128)(2,1)S(1)} %pad_maximum_fusion.34), channel_id=1, source_target_pairs={{0,8},{4,12},{8,0},{12,4},{16,24},{20,28},{24,16},{28,20},{1,9},{5... | collective-permute-start | bytes 786440 | tf_op jit(solution)/shard_map/ppermute | solution.py:293
  156.1 2.4 collective-permute-start.39
  159.4 9.4 %collective-permute-done.39 = bf16[256,256]{1,0:T(8,128)(2,1)S(1)} collective-permute-done((bf16[256,256]{1,0:T(8,128)(2,1)S(1)}, bf16[256,256]{1,0:T(8,128)(2,1)S(1)}, u32[]{:S(2)}, u32[]{:S(2)}) %collective-permute-start.39) | collective-permute-done | bytes 131104 | tf_op jit(solution)/shard_map/ppermute | solution.py:293
  168.8 2.0 collective-permute-done.41
  175.3 2.0 collective-permute-start.25
  182.8 2.6 %collective-permute-done.25 = bf16[512,384]{1,0:T(8,128)(2,1)S(1)} collective-permute-done((bf16[512,384]{1,0:T(8,128)(2,1)S(1)}, bf16[512,384]{1,0:T(8,128)(2,1)S(1)}, u32[]{:S(2)}, u32[]{:S(2)}) %collective-permute-start.25) | collective-permute-done | bytes 393248 | tf_op jit(solution)/shard_map/ppermute | solution.py:280
  186.3 3.1 %collective-permute-done.33 = bf16[512,384]{1,0:T(8,128)(2,1)S(1)} collective-permute-done((bf16[512,384]{1,0:T(8,128)(2,1)S(1)}, bf16[512,384]{1,0:T(8,128)(2,1)S(1)}, u32[]{:S(2)}, u32[]{:S(2)}) %collective-permute-start.33) | collective-permute-done | bytes 393248 | tf_op jit(solution)/shard_map/ppermute | solution.py:280
  190.2 7.5 %collective-permute-done.27 = bf16[512,384]{1,0:T(8,128)(2,1)S(1)} collective-permute-done((bf16[512,384]{1,0:T(8,128)(2,1)S(1)}, bf16[512,384]{1,0:T(8,128)(2,1)S(1)}, u32[]{:S(2)}, u32[]{:S(2)}) %collective-permute-start.27) | collective-permute-done | bytes 393248 | tf_op jit(solution)/shard_map/ppermute | solution.py:280
  198.3 3.0 %collective-permute-done.32 = bf16[256,384]{1,0:T(8,128)(2,1)S(1)} collective-permute-done((bf16[256,384]{1,0:T(8,128)(2,1)S(1)}, bf16[256,384]{1,0:T(8,128)(2,1)S(1)}, u32[]{:S(2)}, u32[]{:S(2)}) %collective-permute-start.32) | collective-permute-done | bytes 196640 | tf_op jit(solution)/shard_map/ppermute | solution.py:280
  204.7 2.4 collective-permute-done.28
  207.7 2.5 %collective-permute-done.35 = bf16[256,384]{1,0:T(8,128)(2,1)S(1)} collective-permute-done((bf16[256,384]{1,0:T(8,128)(2,1)S(1)}, bf16[256,384]{1,0:T(8,128)(2,1)S(1)}, u32[]{:S(2)}, u32[]{:S(2)}) %collective-permute-start.35) | collective-permute-done | bytes 196640 | tf_op jit(solution)/shard_map/ppermute | solution.py:293
  210.3 2.3 collective-permute-start.36
  215.9 2.2 collective-permute-done.36
  218.2 3.0 %collective-permute-done.30 = bf16[256,256]{1,0:T(8,128)(2,1)S(1)} collective-permute-done((bf16[256,256]{1,0:T(8,128)(2,1)S(1)}, bf16[256,256]{1,0:T(8,128)(2,1)S(1)}, u32[]{:S(2)}, u32[]{:S(2)}) %collective-permute-start.30) | collective-permute-done | bytes 131104 | tf_op jit(solution)/shard_map/ppermute | solution.py:293
  223.4 2.0 fusion.7
  231.6 2.5 %collective-permute-done.47 = f32[9,128]{1,0:T(8,128)S(1)} collective-permute-done((f32[9,128]{1,0:T(8,128)S(1)}, f32[9,128]{1,0:T(8,128)S(1)}, u32[]{:S(2)}, u32[]{:S(2)}) %collective-permute-start.47) | collective-permute-done | bytes 4640 | tf_op jit(solution)/shard_map/ppermute | solution.py:280
  235.8 3.6 %collective-permute-done.49 = f32[9,128]{1,0:T(8,128)S(1)} collective-permute-done((f32[9,128]{1,0:T(8,128)S(1)}, f32[9,128]{1,0:T(8,128)S(1)}, u32[]{:S(2)}, u32[]{:S(2)}) %collective-permute-start.49) | collective-permute-done | bytes 4640 | tf_op jit(solution)/shard_map/ppermute | solution.py:503
  240.6 2.1 fusion.11
  (351 shorter events, 97.7 us)
Async XLA Ops:
  2.6 21.5 %collective-permute-start.11 = (bf16[128,1024]{1,0:T(8,128)(2,1)}, bf16[128,1024]{1,0:T(8,128)(2,1)S(1)}, u32[]{:S(2)}, u32[]{:S(2)}) collective-permute-start(bf16[128,1024]{1,0:T(8,128)(2,1)} %slice_select_fusion.4), channel_id=1, source_target_pairs={{0,1},{1,0},{2,3},{3,2},{4,5},{5,4},{6,7},{7,6},{8,9},{9,8},{10,11... | collective-permute-start | bytes 786440 | tf_op jit(solution)/shard_map/ppermute | solution.py:280
  5.6 16.9 %collective-permute-start.9 = (bf16[128,1024]{1,0:T(8,128)(2,1)}, bf16[128,1024]{1,0:T(8,128)(2,1)S(1)}, u32[]{:S(2)}, u32[]{:S(2)}) collective-permute-start(bf16[128,1024]{1,0:T(8,128)(2,1)} %slice_select_fusion.4), channel_id=1, source_target_pairs={{0,2},{1,3},{2,0},{3,1},{4,6},{5,7},{6,4},{7,5},{8,10},{9,11},{10,... | collective-permute-start | bytes 786440 | tf_op jit(solution)/shard_map/ppermute | solution.py:280
  17.2 23.1 %collective-permute-start.14 = (bf16[256,768]{1,0:T(8,128)(2,1)}, bf16[256,768]{1,0:T(8,128)(2,1)S(1)}, u32[]{:S(2)}, u32[]{:S(2)}) collective-permute-start(bf16[256,768]{1,0:T(8,128)(2,1)} %constant_dynamic-update-slice_fusion.13), channel_id=1, source_target_pairs={{0,2},{1,3},{2,0},{3,1},{4,6},{5,7},{6,4},{7,5},{8,10},{9,11},{10,... | collective-permute-start | bytes 1179656 | tf_op jit(solution)/shard_map/ppermute | solution.py:280
  17.7 25.4 %collective-permute-start.13 = (bf16[256,768]{1,0:T(8,128)(2,1)}, bf16[256,768]{1,0:T(8,128)(2,1)S(1)}, u32[]{:S(2)}, u32[]{:S(2)}) collective-permute-start(bf16[256,768]{1,0:T(8,128)(2,1)} %constant_dynamic-update-slice_fusion.13), channel_id=1, source_target_pairs={{0,1},{1,0},{2,3},{3,2},{4,5},{5,4},{6,7},{7,6},{8,9},{9,8},{10,11... | collective-permute-start | bytes 1179656 | tf_op jit(solution)/shard_map/ppermute | solution.py:280
  20.3 20.5 %collective-permute-start.3 = (bf16[256,768]{1,0:T(8,128)(2,1)}, bf16[256,768]{1,0:T(8,128)(2,1)S(1)}, u32[]{:S(2)}, u32[]{:S(2)}) collective-permute-start(bf16[256,768]{1,0:T(8,128)(2,1)} %get-tuple-element.63), channel_id=1, source_target_pairs={{0,2},{1,3},{2,0},{3,1},{4,6},{5,7},{6,4},{7,5},{8,10},{9,11},{10,... | collective-permute-start | bytes 1179656 | tf_op jit(solution)/shard_map/ppermute | solution.py:280
  22.5 8.2 %collective-permute-start.10 = (bf16[64,1024]{1,0:T(8,128)(2,1)S(1)}, bf16[64,1024]{1,0:T(8,128)(2,1)S(1)}, u32[]{:S(2)}, u32[]{:S(2)}) collective-permute-start(bf16[64,1024]{1,0:T(8,128)(2,1)S(1)} %slice.503), channel_id=1, source_target_pairs={{0,1},{1,0},{2,3},{3,2},{4,5},{5,4},{6,7},{7,6},{8,9},{9,8},{10,11... | collective-permute-start | bytes 393224 | tf_op jit(solution)/shard_map/ppermute | solution.py:280
  24.8 14.1 %collective-permute-start.12 = (bf16[64,1024]{1,0:T(8,128)(2,1)}, bf16[64,1024]{1,0:T(8,128)(2,1)S(1)}, u32[]{:S(2)}, u32[]{:S(2)}) collective-permute-start(bf16[64,1024]{1,0:T(8,128)(2,1)} %slice.504), channel_id=1, source_target_pairs={{0,2},{1,3},{2,0},{3,1},{4,6},{5,7},{6,4},{7,5},{8,10},{9,11},{10,... | collective-permute-start | bytes 393224 | tf_op jit(solution)/shard_map/ppermute | solution.py:280
  30.7 10.8 %collective-permute-start.2 = (bf16[256,768]{1,0:T(8,128)(2,1)}, bf16[256,768]{1,0:T(8,128)(2,1)S(1)}, u32[]{:S(2)}, u32[]{:S(2)}) collective-permute-start(bf16[256,768]{1,0:T(8,128)(2,1)} %get-tuple-element.63), channel_id=1, source_target_pairs={{0,1},{1,0},{2,3},{3,2},{4,5},{5,4},{6,7},{7,6},{8,9},{9,8},{10,11... | collective-permute-start | bytes 1179656 | tf_op jit(solution)/shard_map/ppermute | solution.py:280
  38.9 19.5 %collective-permute-start.1 = (bf16[384,1024]{1,0:T(8,128)(2,1)S(1)}, bf16[384,1024]{1,0:T(8,128)(2,1)S(1)}, u32[]{:S(2)}, u32[]{:S(2)}) collective-permute-start(bf16[384,1024]{1,0:T(8,128)(2,1)S(1)} %bitcast.117), channel_id=1, source_target_pairs={{0,4},{4,0},{8,12},{12,8},{16,20},{20,16},{24,28},{28,24},{1,5},{5... | collective-permute-start | bytes 2359304 | tf_op jit(solution)/shard_map/ppermute | solution.py:370
  40.3 35.2 %collective-permute-start.8 = (bf16[384,1024]{1,0:T(8,128)(2,1)S(1)}, bf16[384,1024]{1,0:T(8,128)(2,1)S(1)}, u32[]{:S(2)}, u32[]{:S(2)}) collective-permute-start(bf16[384,1024]{1,0:T(8,128)(2,1)S(1)} %bitcast.122), channel_id=1, source_target_pairs={{0,4},{4,0},{8,12},{12,8},{16,20},{20,16},{24,28},{28,24},{1,5},{5... | collective-permute-start | bytes 2359304 | tf_op jit(solution)/shard_map/ppermute | solution.py:371
  40.9 11.7 %collective-permute-start.15 = (bf16[128,768]{1,0:T(8,128)(2,1)S(1)}, bf16[128,768]{1,0:T(8,128)(2,1)S(1)}, u32[]{:S(2)}, u32[]{:S(2)}) collective-permute-start(bf16[128,768]{1,0:T(8,128)(2,1)S(1)} %slice.505), channel_id=1, source_target_pairs={{0,1},{1,0},{2,3},{3,2},{4,5},{5,4},{6,7},{7,6},{8,9},{9,8},{10,11... | collective-permute-start | bytes 589832 | tf_op jit(solution)/shard_map/ppermute | solution.py:280
  41.5 10.5 %collective-permute-start.4 = (bf16[128,768]{1,0:T(8,128)(2,1)S(1)}, bf16[128,768]{1,0:T(8,128)(2,1)S(1)}, u32[]{:S(2)}, u32[]{:S(2)}) collective-permute-start(bf16[128,768]{1,0:T(8,128)(2,1)S(1)} %slice.499), channel_id=1, source_target_pairs={{0,1},{1,0},{2,3},{3,2},{4,5},{5,4},{6,7},{7,6},{8,9},{9,8},{10,11... | collective-permute-start | bytes 589832 | tf_op jit(solution)/shard_map/ppermute | solution.py:280
  43.1 9.4 %collective-permute-start.5 = (bf16[128,768]{1,0:T(8,128)(2,1)S(1)}, bf16[128,768]{1,0:T(8,128)(2,1)S(1)}, u32[]{:S(2)}, u32[]{:S(2)}) collective-permute-start(bf16[128,768]{1,0:T(8,128)(2,1)S(1)} %slice.500), channel_id=1, source_target_pairs={{0,2},{1,3},{2,0},{3,1},{4,6},{5,7},{6,4},{7,5},{8,10},{9,11},{10,... | collective-permute-start | bytes 589832 | tf_op jit(solution)/shard_map/ppermute | solution.py:280
  62.1 46.8 %collective-permute-start.7 = (bf16[192,512]{1,0:T(8,128)(2,1)}, bf16[192,512]{1,0:T(8,128)(2,1)S(1)}, u32[]{:S(2)}, u32[]{:S(2)}) collective-permute-start(bf16[192,512]{1,0:T(8,128)(2,1)} %get-tuple-element.75), channel_id=1, source_target_pairs={{8,0},{12,4},{16,8},{20,12},{24,16},{28,20},{9,1},{13,5},{17,9},{2... | collective-permute-start | bytes 589832 | tf_op jit(solution)/shard_map/ppermute | solution.py:409
  63.4 46.2 %collective-permute-start.6 = (bf16[192,512]{1,0:T(8,128)(2,1)}, bf16[192,512]{1,0:T(8,128)(2,1)S(1)}, u32[]{:S(2)}, u32[]{:S(2)}) collective-permute-start(bf16[192,512]{1,0:T(8,128)(2,1)} %get-tuple-element.76), channel_id=1, source_target_pairs={{0,8},{4,12},{8,16},{12,20},{16,24},{20,28},{1,9},{5,13},{9,17},{1... | collective-permute-start | bytes 589832 | tf_op jit(solution)/shard_map/ppermute | solution.py:408
  97.4 50.6 %collective-permute-start.22 = (bf16[2,192,256]{2,1,0:T(8,128)(2,1)}, bf16[2,192,256]{2,1,0:T(8,128)(2,1)}, u32[]{:S(2)}, u32[]{:S(2)}) collective-permute-start(bf16[2,192,256]{2,1,0:T(8,128)(2,1)} %get-tuple-element.29), channel_id=1, source_target_pairs={{0,8},{4,12},{8,16},{12,20},{16,24},{20,28},{1,9},{5,13},{9,17},{1... | collective-permute-start | bytes 589832 | tf_op jit(solution)/shard_map/ppermute | solution.py:424
  102.5 47.2 %collective-permute-start.23 = (bf16[2,192,256]{2,1,0:T(8,128)(2,1)}, bf16[2,192,256]{2,1,0:T(8,128)(2,1)}, u32[]{:S(2)}, u32[]{:S(2)}) collective-permute-start(bf16[2,192,256]{2,1,0:T(8,128)(2,1)} %get-tuple-element.30), channel_id=1, source_target_pairs={{8,0},{12,4},{16,8},{20,12},{24,16},{28,20},{9,1},{13,5},{17,9},{2... | collective-permute-start | bytes 589832 | tf_op jit(solution)/shard_map/ppermute | solution.py:423
  131.2 13.2 %collective-permute-start.20 = (bf16[2,192,256]{2,1,0:T(8,128)(2,1)}, bf16[2,192,256]{2,1,0:T(8,128)(2,1)S(1)}, u32[]{:S(2)}, u32[]{:S(2)}) collective-permute-start(bf16[2,192,256]{2,1,0:T(8,128)(2,1)} %copy-done.11), channel_id=1, source_target_pairs={{0,8},{4,12},{8,16},{12,20},{16,24},{20,28},{1,9},{5,13},{9,17},{1... | collective-permute-start | bytes 589832 | tf_op jit(solution)/shard_map/ppermute | solution.py:424
  135.9 9.4 %collective-permute-start.21 = (bf16[2,192,256]{2,1,0:T(8,128)(2,1)}, bf16[2,192,256]{2,1,0:T(8,128)(2,1)S(1)}, u32[]{:S(2)}, u32[]{:S(2)}) collective-permute-start(bf16[2,192,256]{2,1,0:T(8,128)(2,1)} %copy-done.10), channel_id=1, source_target_pairs={{8,0},{12,4},{16,8},{20,12},{24,16},{28,20},{9,1},{13,5},{17,9},{2... | collective-permute-start | bytes 589832 | tf_op jit(solution)/shard_map/ppermute | solution.py:423
  139.8 16.1 %collective-permute-start.38 = (bf16[256,512]{1,0:T(8,128)(2,1)S(1)}, bf16[256,512]{1,0:T(8,128)(2,1)S(1)}, u32[]{:S(2)}, u32[]{:S(2)}) collective-permute-start(bf16[256,512]{1,0:T(8,128)(2,1)S(1)} %pad_maximum_fusion.34), channel_id=1, source_target_pairs={{0,8},{4,12},{8,0},{12,4},{16,24},{20,28},{24,16},{28,20},{1,9},{5... | collective-permute-start | bytes 786440 | tf_op jit(solution)/shard_map/ppermute | solution.py:293
  144.4 14.1 %collective-permute-start.40 = (bf16[256,512]{1,0:T(8,128)(2,1)S(1)}, bf16[256,512]{1,0:T(8,128)(2,1)S(1)}, u32[]{:S(2)}, u32[]{:S(2)}) collective-permute-start(bf16[256,512]{1,0:T(8,128)(2,1)S(1)} %pad_maximum_fusion.35), channel_id=1, source_target_pairs={{0,8},{4,12},{8,0},{12,4},{16,24},{20,28},{24,16},{28,20},{1,9},{5... | collective-permute-start | bytes 786440 | tf_op jit(solution)/shard_map/ppermute | solution.py:293
  145.4 77.1 %collective-permute-start.19 = (f32[384,1024]{1,0:T(8,128)S(1)}, f32[384,1024]{1,0:T(8,128)S(1)}, u32[]{:S(2)}, u32[]{:S(2)}) collective-permute-start(f32[384,1024]{1,0:T(8,128)S(1)} %constant_dynamic-slice_fusion.1), channel_id=1, source_target_pairs={{0,4},{4,0},{8,12},{12,8},{16,20},{20,16},{24,28},{28,24},{1,5},{5... | collective-permute-start | bytes 4718600 | tf_op jit(solution)/shard_map/ppermute | solution.py:472
  148.0 34.4 %collective-permute-start.31 = (bf16[512,384]{1,0:T(8,128)(2,1)S(1)}, bf16[512,384]{1,0:T(8,128)(2,1)S(1)}, u32[]{:S(2)}, u32[]{:S(2)}) collective-permute-start(bf16[512,384]{1,0:T(8,128)(2,1)S(1)} %convolution_convert_fusion.4), channel_id=1, source_target_pairs={{0,1},{1,0},{2,3},{3,2},{4,5},{5,4},{6,7},{7,6},{8,9},{9,8},{10,11... | collective-permute-start | bytes 1179656 | tf_op jit(solution)/shard_map/ppermute | solution.py:280
  156.1 12.6 %collective-permute-start.39 = (bf16[256,256]{1,0:T(8,128)(2,1)S(1)}, bf16[256,256]{1,0:T(8,128)(2,1)S(1)}, u32[]{:S(2)}, u32[]{:S(2)}) collective-permute-start(bf16[256,256]{1,0:T(8,128)(2,1)S(1)} %get-tuple-element.39), channel_id=1, source_target_pairs={{0,16},{4,20},{8,24},{12,28},{16,0},{20,4},{24,8},{28,12},{1,17},{... | collective-permute-start | bytes 393224 | tf_op jit(solution)/shard_map/ppermute | solution.py:293
  158.7 12.1 %collective-permute-start.41 = (bf16[256,256]{1,0:T(8,128)(2,1)S(1)}, bf16[256,256]{1,0:T(8,128)(2,1)S(1)}, u32[]{:S(2)}, u32[]{:S(2)}) collective-permute-start(bf16[256,256]{1,0:T(8,128)(2,1)S(1)} %get-tuple-element.36), channel_id=1, source_target_pairs={{0,16},{4,20},{8,24},{12,28},{16,0},{20,4},{24,8},{28,12},{1,17},{... | collective-permute-start | bytes 393224 | tf_op jit(solution)/shard_map/ppermute | solution.py:293
  175.3 10.2 %collective-permute-start.25 = (bf16[512,384]{1,0:T(8,128)(2,1)S(1)}, bf16[512,384]{1,0:T(8,128)(2,1)S(1)}, u32[]{:S(2)}, u32[]{:S(2)}) collective-permute-start(bf16[512,384]{1,0:T(8,128)(2,1)S(1)} %convolution_convert_fusion.6), channel_id=1, source_target_pairs={{0,1},{1,0},{2,3},{3,2},{4,5},{5,4},{6,7},{7,6},{8,9},{9,8},{10,11... | collective-permute-start | bytes 1179656 | tf_op jit(solution)/shard_map/ppermute | solution.py:280
  177.3 12.1 %collective-permute-start.33 = (bf16[512,384]{1,0:T(8,128)(2,1)S(1)}, bf16[512,384]{1,0:T(8,128)(2,1)S(1)}, u32[]{:S(2)}, u32[]{:S(2)}) collective-permute-start(bf16[512,384]{1,0:T(8,128)(2,1)S(1)} %convolution_convert_fusion.3), channel_id=1, source_target_pairs={{0,2},{1,3},{2,0},{3,1},{4,6},{5,7},{6,4},{7,5},{8,10},{9,11},{10,... | collective-permute-start | bytes 1179656 | tf_op jit(solution)/shard_map/ppermute | solution.py:280
  180.3 17.5 %collective-permute-start.27 = (bf16[512,384]{1,0:T(8,128)(2,1)S(1)}, bf16[512,384]{1,0:T(8,128)(2,1)S(1)}, u32[]{:S(2)}, u32[]{:S(2)}) collective-permute-start(bf16[512,384]{1,0:T(8,128)(2,1)S(1)} %convolution_convert_fusion.5), channel_id=1, source_target_pairs={{0,2},{1,3},{2,0},{3,1},{4,6},{5,7},{6,4},{7,5},{8,10},{9,11},{10,... | collective-permute-start | bytes 1179656 | tf_op jit(solution)/shard_map/ppermute | solution.py:280
  182.4 39.5 %collective-permute-start.24 = (f32[384,1024]{1,0:T(8,128)S(1)}, f32[384,1024]{1,0:T(8,128)S(1)}, u32[]{:S(2)}, u32[]{:S(2)}) collective-permute-start(f32[384,1024]{1,0:T(8,128)S(1)} %constant_dynamic-slice_fusion), channel_id=1, source_target_pairs={{0,4},{4,0},{8,12},{12,8},{16,20},{20,16},{24,28},{28,24},{1,5},{5... | collective-permute-start | bytes 4718600 | tf_op jit(solution)/shard_map/ppermute | solution.py:477
  185.4 16.0 %collective-permute-start.32 = (bf16[256,384]{1,0:T(8,128)(2,1)S(1)}, bf16[256,384]{1,0:T(8,128)(2,1)S(1)}, u32[]{:S(2)}, u32[]{:S(2)}) collective-permute-start(bf16[256,384]{1,0:T(8,128)(2,1)S(1)} %fusion.42), channel_id=1, source_target_pairs={{0,2},{1,3},{2,0},{3,1},{4,6},{5,7},{6,4},{7,5},{8,10},{9,11},{10,... | collective-permute-start | bytes 589832 | tf_op jit(solution)/shard_map/ppermute | solution.py:280
  189.4 14.9 %collective-permute-start.26 = (bf16[256,384]{1,0:T(8,128)(2,1)S(1)}, bf16[256,384]{1,0:T(8,128)(2,1)S(1)}, u32[]{:S(2)}, u32[]{:S(2)}) collective-permute-start(bf16[256,384]{1,0:T(8,128)(2,1)S(1)} %fusion.41), channel_id=1, source_target_pairs={{0,2},{1,3},{2,0},{3,1},{4,6},{5,7},{6,4},{7,5},{8,10},{9,11},{10,... | collective-permute-start | bytes 589832 | tf_op jit(solution)/shard_map/ppermute | solution.py:280
  210.3 7.9 %collective-permute-start.36 = (bf16[256,256]{1,0:T(8,128)(2,1)S(1)}, bf16[256,256]{1,0:T(8,128)(2,1)S(1)}, u32[]{:S(2)}, u32[]{:S(2)}) collective-permute-start(bf16[256,256]{1,0:T(8,128)(2,1)S(1)} %select_convert_fusion.8), channel_id=1, source_target_pairs={{0,16},{4,20},{8,24},{12,28},{16,0},{20,4},{24,8},{28,12},{1,17},{... | collective-permute-start | bytes 393224 | tf_op jit(solution)/shard_map/ppermute | solution.py:293
  (82 other events, 673.8 us)

commit v3 on v2

--- a/solution.py
+++ b/solution.py
@@ -38,13 +38,14 @@
 
 
 def attention_kernel(
-    mult_ref, valid_ref, scale_ref,
-    q_ref, k_ref, v_ref, kb_ref, vb_ref, ka_ref, va_ref, u_ref,
-    att_ref, dq_ref, dk_ref, dv_ref, rim_b_ref, rim_a_ref, ds_ref,
+    mult_ref, valid_ref, scale_ref, even_ref,
+    q_ref, k_ref, v_ref, k1_ref, v1_ref, k2_ref, v2_ref, u_ref,
+    att_ref, dq_ref, dk_ref, dv_ref, rim1_ref, rim2_ref, ds_ref,
     k_unit, k_len, k_low, k_turn, v_low, v_turn, mult, s_ref, g_ref, e_ref, w_low, c_low, dk, dv,
 ):
     rows = q_ref.shape[0]
-    margin = kb_ref.shape[0]
+    margin = k1_ref.shape[0]
+    even = even_ref[0] == 1
     pool = rows + 2 * margin
     reach = margin // BLK
     steps = rows // PAIR
@@ -71,17 +72,23 @@
             [jnp.where(first_lanes, x, 0.0), jnp.where(first_lanes, 0.0, x)], axis=0
         ).astype(BF)
 
-    for src_k, src_v, at, count in (
-        (kb_ref, vb_ref, 0, margin), (k_ref, v_ref, margin, rows), (ka_ref, va_ref, margin + rows, margin)
-    ):
-        for part in range(0, count, 128 if count % 128 == 0 else 64):
-            size = 128 if count % 128 == 0 else 64
-            place = slice(at + part, at + part + size)
-            unit, length = unit_rows(src_k[part : part + size, :].astype(F32), same_head)
-            k_unit[place, :] = unit
-            k_len[place, :] = length
-            k_low[place, :] = unit.astype(BF)
-            v_low[place, :] = src_v[part : part + size, :]
+    def take(at, keys, values):
+        unit, length = unit_rows(keys.astype(F32), same_head)
+        place = slice(at, at + keys.shape[0])
+        k_unit[place, :] = unit
+        k_len[place, :] = length
+        k_low[place, :] = unit.astype(BF)
+        v_low[place, :] = values
+
+    for part in range(0, margin, BLK):
+        here = slice(part, part + BLK)
+        k1, k2 = k1_ref[here, :].astype(F32), k2_ref[here, :].astype(F32)
+        v1, v2 = v1_ref[here, :].astype(F32), v2_ref[here, :].astype(F32)
+        take(part, jnp.where(even, k2, k1), jnp.where(even, v2, v1).astype(BF))
+        take(margin + rows + part, jnp.where(even, k1, k2), jnp.where(even, v1, v2).astype(BF))
+    for part in range(0, rows, PAIR):
+        here = slice(part, part + PAIR)
+        take(margin + part, k_ref[here, :], v_ref[here, :])
     for part in range(0, pool, 128):
         place = slice(part, part + 128)
         k_turn[:, place] = jnp.transpose(k_low[place, :].astype(F32)).astype(BF)
@@ -146,33 +153,35 @@
         dv[window, :] += dot(w_low[...], u_split)
         dk[window, :] += dot(c_low[...], q_split)
 
-    for part in range(0, pool, 64):
-        place = slice(part, part + 64)
-        grad_k = unit_back(k_unit[place, :], k_len[place, :], dk[place, :], same_head)
-        grad_v = dv[place, :]
-        if part < margin:
-            rim_b_ref[0, place, :] = grad_k.astype(BF)
-            rim_b_ref[1, place, :] = grad_v.astype(BF)
-        elif part < margin + rows:
-            here = slice(part - margin, part - margin + 64)
-            dk_ref[here, :] = grad_k
-            dv_ref[here, :] = grad_v
-        else:
-            here = slice(part - margin - rows, part - margin - rows + 64)
-            rim_a_ref[0, here, :] = grad_k.astype(BF)
-            rim_a_ref[1, here, :] = grad_v.astype(BF)
+    def key_grad(part):
+        place = slice(part, part + BLK)
+        return unit_back(k_unit[place, :], k_len[place, :], dk[place, :], same_head)
+
+    for part in range(0, rows, BLK):
+        here = slice(part, part + BLK)
+        dk_ref[here, :] = key_grad(margin + part)
+        dv_ref[here, :] = dv[margin + part : margin + part + BLK, :]
+    for part in range(0, margin, BLK):
+        here = slice(part, part + BLK)
+        far = margin + rows + part
+        kb, ka = key_grad(part), key_grad(far)
+        vb, va = dv[part : part + BLK, :], dv[far : far + BLK, :]
+        rim1_ref[0, here, :] = jnp.where(even, ka, kb).astype(BF)
+        rim1_ref[1, here, :] = jnp.where(even, va, vb).astype(BF)
+        rim2_ref[0, here, :] = jnp.where(even, kb, ka).astype(BF)
+        rim2_ref[1, here, :] = jnp.where(even, vb, va).astype(BF)
     ds_ref[0, :, :] = ds
 
 
-def attention(packed, before, after, upstream, mult, valid, scales, pairs):
+def attention(packed, first, second, upstream, mult, valid, scales, even, pairs):
     rows, width3 = packed.shape
     width = width3 // 3
-    margin = before.shape[0]
+    margin = first.shape[0]
     pool = rows + 2 * margin
     count = len(pairs)
+    stride = pairs[1] - pairs[0]
     steps = rows // PAIR
     span = WINDOW * BLK
-    first, stride = pairs[0], pairs[1] - pairs[0]
 
     def at(offset):
         return lambda p, *_: (0, offset + p)
@@ -180,7 +189,7 @@
     return pl.pallas_call(
         attention_kernel,
         grid_spec=pltpu.PrefetchScalarGridSpec(
-            num_scalar_prefetch=3,
+            num_scalar_prefetch=4,
             grid=(count,),
             in_specs=[
                 pl.BlockSpec((rows, PAIR), at(0)),
@@ -190,7 +199,7 @@
                 pl.BlockSpec((margin, PAIR), at(count)),
                 pl.BlockSpec((margin, PAIR), at(0)),
                 pl.BlockSpec((margin, PAIR), at(count)),
-                pl.BlockSpec((rows, PAIR), lambda p, *_: (0, first + stride * p)),
+                pl.BlockSpec((rows, PAIR), lambda p, *_: (0, pairs[0] + stride * p)),
             ],
             out_specs=[
                 pl.BlockSpec((rows, PAIR), at(0)),
@@ -230,11 +239,57 @@
         compiler_params=pltpu.CompilerParams(vmem_limit_bytes=40 * 1024 * 1024),
         cost_estimate=pl.CostEstimate(
             flops=8 * 2 * 6 * count * steps * span * 256 * 128,
-            bytes_accessed=packed.size * 2 + rows * width * 14,
+            bytes_accessed=rows * width * 20,
             transcendentals=count * steps * span * 256,
         ),
         name="block_attention",
-    )(mult, valid, scales, packed, packed, packed, before, before, after, after, upstream)
+    )(mult, valid, scales, even, packed, packed, packed, first, first, second, second, upstream)
+
+
+def pick_kernel(core_ref, qkv_ref, out_ref, first_ref, second_ref):
+    core = core_ref[0]
+    for ref, pairs in zip((first_ref, second_ref), CHUNKS):
+        at = 0
+        for base in range(0, qkv_ref.shape[1], 8 * PAIR):
+            for p in pairs:
+                start = pl.multiple_of(base + 2 * p * PAIR + core * PAIR, PAIR)
+                ref[:, at : at + PAIR] = qkv_ref[:, pl.ds(start, PAIR)]
+                at += PAIR
+    half = out_ref.shape[1] // 2
+    rows = out_ref[pl.ds(pl.multiple_of(core * PAIR, PAIR), PAIR), :]
+    first_ref[:PAIR, at:] = rows[:, :half]
+    first_ref[PAIR:, at:] = rows[:, half:]
+
+
+def pick_weights(w_qkv, w_out, core):
+    height, columns = w_qkv.shape
+    part = columns // 4
+    wide = part + w_out.shape[1] // 2
+    return pl.pallas_call(
+        pick_kernel,
+        grid_spec=pltpu.PrefetchScalarGridSpec(
+            num_scalar_prefetch=1,
+            grid=(1,),
+            in_specs=[
+                pl.BlockSpec(w_qkv.shape, lambda i, *_: (0, 0)),
+                pl.BlockSpec(w_out.shape, lambda i, *_: (0, 0)),
+            ],
+            out_specs=[
+                pl.BlockSpec((height, wide), lambda i, *_: (0, 0)),
+                pl.BlockSpec((height, part), lambda i, *_: (0, 0)),
+            ],
+        ),
+        out_shape=[
+            jax.ShapeDtypeStruct((height, wide), BF),
+            jax.ShapeDtypeStruct((height, part), BF),
+        ],
+        compiler_params=pltpu.CompilerParams(vmem_limit_bytes=16 * 1024 * 1024),
+        name="pick_weights",
+    )(jnp.reshape(core, (1,)).astype(jnp.int32), w_qkv, w_out)
+
+
+def gate(value, *others):
+    return lax.optimization_barrier((value,) + others)[0]
 
 
 def pick_groups(array, axis, unit, core):
@@ -280,39 +335,57 @@
     return lax.ppermute(value, "fsdp", [(i, i ^ step) for i in range(4)])
 
 
-def gather_square(shard):
-    half = shard.shape[0] // 2
-    near = square(shard, 1)
-    far = square(shard, 2)
+def gather_near(shard):
+    return square(shard, 1), square(shard, 2)
+
+
+def gather_far(near, far):
+    half = near.shape[0] // 2
     top = square(far[:half], 1)
     low = square(near[half:], 2)
-    return [near, jnp.concatenate([top, low], axis=0), far, shard]
+    return jnp.concatenate([top, low], axis=0)
 
 
 def chips(value, step, n_vox):
     return lax.ppermute(value, "vox", [(i, i ^ (2 * step)) for i in range(n_vox)])
 
 
-def reduce_square(normed_blocks, grad):
+def stacked(block):
+    half = block.shape[1] // 2
+    return jnp.concatenate([block[:, :half], block[:, half:]], axis=0)
+
+
+def reduce_terms(normed, grad, place, side, extra=None):
     half = grad.shape[1] // 2
-    one, three, two, zero = normed_blocks
-    left, right = grad[:, :half], grad[:, half:]
-    t = ((0,), (0,))
-
-    def both(a, b):
-        return jnp.concatenate([a, b], axis=1)
-
-    got_left = square(dot(both(one, three), left, t).astype(BF), 1)
-    got_right = square(dot(both(three, two), right, t).astype(BF), 2)
-    size = zero.shape[1]
-    pass_left = dot(two, left, t) + got_left[size:].astype(F32)
-    pass_right = dot(one, right, t) + got_right[:size].astype(F32)
-    end_left = square(pass_left.astype(BF), 2)
-    end_right = square(pass_right.astype(BF), 1)
-    kept_left = dot(zero, left, t) + got_left[:size].astype(F32)
-    kept_right = dot(zero, right, t) + got_right[size:].astype(F32)
-    return jnp.concatenate(
-        [kept_left + end_left.astype(F32), kept_right + end_right.astype(F32)], axis=1
+    size = normed.shape[1] // 4
+    columns = grad[:, side * half : (side + 1) * half]
+    value = dot(normed[:, place.start * size : place.stop * size], columns, ((0,), (0,)))
+    if extra is None:
+        return value
+    more = jnp.concatenate([extra[k] for k in range(place.start, place.stop)], axis=0)
+    half = more.shape[1] // 2
+    return jnp.concatenate([value, more[:, side * half : (side + 1) * half]], axis=1)
+
+
+def reduce_first(normed, grad, extra=None):
+    return (
+        reduce_terms(normed, grad, slice(0, 2), 0, extra).astype(BF),
+        reduce_terms(normed, grad, slice(1, 3), 1, extra).astype(BF),
+    )
+
+
+def reduce_second(normed, grad, from_x, from_y, extra=None):
+    size = normed.shape[1] // 4
+    to_y = reduce_terms(normed, grad, slice(2, 3), 0, extra) + from_x[size:].astype(F32)
+    to_x = reduce_terms(normed, grad, slice(0, 1), 1, extra) + from_y[:size].astype(F32)
+    return to_x.astype(BF), to_y.astype(BF)
+
+
+def reduce_kept(normed, grad, from_x, from_y, extra=None):
+    size = normed.shape[1] // 4
+    return (
+        reduce_terms(normed, grad, slice(3, 4), 0, extra) + from_x[:size].astype(F32),
+        reduce_terms(normed, grad, slice(3, 4), 1, extra) + from_y[size:].astype(F32),
     )
 
 
@@ -338,8 +411,13 @@
     fast = n_vox == 8 and n_fsdp == 4
     unit = 128 if fast else 64
     swap = [(i, i ^ 1) for i in range(n_vox)]
-    up = [(i, i + 2) for i in range(n_vox - 2)]
-    down = [(j, i) for i, j in up]
+    even, low = chip % 2 == 0, chip < 2
+    even_flag = jnp.reshape(even, (1,)).astype(jnp.int32)
+    near_chips = [(i, i ^ 2) for i in range(n_vox)]
+    far_chips = []
+    for i in range(n_vox):
+        to = i // 2 + (1 if i // 2 % 2 else -1)
+        far_chips.append((i, 2 * to + i % 2 if 0 <= to < n_chip else i))
     part_width = model_width // 2
 
     def columns_of(array, pairs):
@@ -352,16 +430,24 @@
             axis=1,
         )
 
-    core_qkv = pick_groups(w_qkv, 1, unit, core)
-    core_out = pick_groups(w_out, 0, unit, core)
     if fast:
-        qkv_chunks = [
-            jnp.concatenate(gather_square(columns_of(core_qkv, pairs)), axis=0) for pairs in CHUNKS
+        shard, shard_1 = pick_weights(w_qkv, w_out, core)
+        near, far = gather_near(shard)
+        diag = gather_far(near, far)
+        weights_1 = lax.all_gather(gate(shard_1, near, far), "fsdp", axis=0, tiled=True)
+        turned = xor_blocks(jnp.split(weights_1, 4, axis=0), scene)
+        weights_1 = jnp.concatenate([turned[k] for k in ORDER], axis=0)
+        wide = shard_1.shape[1]
+        weights_0 = jnp.concatenate([block[:, :wide] for block in (near, diag, far, shard)], axis=0)
+        out_blocks = [
+            jnp.concatenate([block[:PAIR, wide:], block[PAIR:, wide:]], axis=1)
+            for block in (shard, near, far, diag)
         ]
-        one, three, two, zero = gather_square(core_out)
-        out_half = jnp.concatenate(xor_blocks([zero, one, two, three], scene), axis=0)
+        out_half = jnp.concatenate(xor_blocks(out_blocks, scene), axis=0)
     else:
-        qkv_chunks = [
+        core_qkv = pick_groups(w_qkv, 1, unit, core)
+        core_out = pick_groups(w_out, 0, unit, core)
+        weights_0, weights_1 = [
             lax.all_gather(columns_of(core_qkv, pairs), "fsdp", axis=0, tiled=True)
             for pairs in CHUNKS
         ]
@@ -398,73 +484,120 @@
     normed = (wide * inverse * gain).astype(BF)
     if fast:
         turned = xor_blocks(jnp.split(normed, 4, axis=1), scene)
-        normed_blocks = [turned[k] for k in ORDER]
-        normed = jnp.concatenate(normed_blocks, axis=1)
-
-    packed_chunks, halos = [], []
-    for weight in qkv_chunks:
+        normed = jnp.concatenate([turned[k] for k in ORDER], axis=1)
+
+    def pairings(first, second):
+        return lax.ppermute(first, "vox", near_chips), lax.ppermute(second, "vox", far_chips)
+
+    def project(weight):
         packed = dot(normed, weight).astype(BF)
         width = packed.shape[1] // 3
-        before = lax.ppermute(packed[rows - margin :, width:], "vox", up)
-        after = lax.ppermute(packed[:margin, width:], "vox", down)
-        packed_chunks.append(packed)
-        halos.append((before, after))
+        top, bottom = packed[:margin, width:], packed[rows - margin :, width:]
+        return (packed,) + pairings(jnp.where(even, bottom, top), jnp.where(even, top, bottom))
+
+    def heads_of(inputs, upstream, pairs):
+        chunk_scales = jnp.concatenate([scales[2 * p : 2 * p + 2] for p in pairs])
+        return attention(*inputs, upstream, mult, valid, chunk_scales, even_flag, pairs)
+
+    def with_rims(grad, first, second):
+        first, second = first.astype(F32), second.astype(F32)
+        return jnp.concatenate(
+            [
+                grad[:margin] + jnp.where(even, second, first),
+                grad[margin : rows - margin],
+                grad[rows - margin :] + jnp.where(even, first, second),
+            ],
+            axis=0,
+        ).astype(BF)
+
+    def gradients(result, rims):
+        return jnp.concatenate(
+            [result[1]]
+            + [with_rims(result[2 + i], rims[0][i], rims[1][i]) for i in range(2)],
+            axis=1,
+        )
+
+    def out_rows(pairs):
+        return jnp.concatenate([out_half[p * PAIR : (p + 1) * PAIR] for p in pairs], axis=0)
+
+    def groups_of(left, right, chunk):
+        half = 3 * PAIR
+        groups = [left[:, k * PAIR : (k + 1) * PAIR] for k in range(3)]
+        groups += [right[:, k * PAIR : (k + 1) * PAIR] for k in range(3)]
+        sets = ((0, 3, 4), (1, 2, 5)) if chunk == 0 else ((0, 1, 3), (2, 4, 5))
+        evens = jnp.concatenate([groups[k] for k in sets[0]] + [left[:, half:]], axis=1)
+        odds = jnp.concatenate([groups[k] for k in sets[1]] + [right[:, half:]], axis=1)
+        return jnp.where(even, evens, odds), jnp.where(even, odds, evens).astype(BF)
+
+    def halves_of(kept):
+        left, right = kept[:, : 2 * PAIR], kept[:, PAIR : 3 * PAIR]
+        if kept.shape[1] > 3 * PAIR:
+            more = kept[:, 3 * PAIR :]
+            cut = more.shape[0] // 2
+            left = jnp.concatenate([left, more[:cut]], axis=0)
+            right = jnp.concatenate([right, more[cut:]], axis=0)
+        return jnp.where(low, left, right), jnp.where(low, right, left).astype(BF)
+
+    packed_0 = project(weights_0)
     upstream = dot(chip_cotangent, out_half, ((1,), (1,))).astype(BF)
-
-    mixed_part = 0.0
-    ngrad_part = 0.0
+    first = heads_of(packed_0, upstream, CHUNKS[0])
+    rims_0 = pairings(first[4], first[5])
+    packed_1 = project(gate(weights_1, first[4], first[5]) if fast else weights_1)
+    out_grad_0 = dot(first[0], chip_cotangent, ((0,), (0,)))
+    mixed_0 = dot(first[0], out_rows(CHUNKS[0]))
+    grad_0 = gradients(first, rims_0)
+    if fast:
+        to_x, to_y = reduce_first(normed, grad_0)
+        from_x0, from_y0 = square(to_x, 1), square(to_y, 2)
+        second_in = gate(upstream, to_x, to_y, out_grad_0, mixed_0)
+    else:
+        second_in = upstream
+    second = heads_of(packed_1, second_in, CHUNKS[1])
+    rims_1 = pairings(second[4], second[5])
+    grad_1 = gradients(second, rims_1)
+    out_grad_1 = dot(second[0], chip_cotangent, ((0,), (0,)))
+    mixed_part = mixed_0 + dot(second[0], out_rows(CHUNKS[1]))
+    if fast:
+        grad_0 = gate(grad_0, second[4], second[5])
+        to_x, to_y = reduce_second(normed, grad_0, from_x0, from_y0)
+        end_x, end_y = square(to_x, 1), square(to_y, 2)
+        left, right = reduce_kept(normed, grad_0, from_x0, from_y0)
+        blocks_of = {}
+        for pairs, value in zip(CHUNKS, (out_grad_0, out_grad_1)):
+            for i, p in enumerate(pairs):
+                blocks_of[p] = value[i * PAIR : (i + 1) * PAIR]
+        turned = xor_blocks([blocks_of[p] for p in range(4)], scene)
+        extra = [stacked(turned[k]) for k in ORDER]
+        to_x, to_y = reduce_first(normed, grad_1, extra)
+        from_x1, from_y1 = square(to_x, 1), square(to_y, 2)
+        left, right = left + end_y.astype(F32), right + end_x.astype(F32)
+        left, right, grad_0, grad_1, mixed_part, _, _ = lax.optimization_barrier(
+            (left, right, grad_0, grad_1, mixed_part, to_x, to_y)
+        )
+        kept_0, sent = groups_of(left, right, 0)
+        got = chips(sent, 1, n_vox)
+        ngrad_part = dot(grad_0, weights_0, ((1,), (1,))) + dot(grad_1, weights_1, ((1,), (1,)))
+        to_x, to_y = reduce_second(normed, grad_1, from_x1, from_y1, extra)
+        end_x, end_y = square(to_x, 1), square(to_y, 2)
+        left, right = reduce_kept(normed, grad_1, from_x1, from_y1, extra)
+        kept_0, sent = halves_of(gate(kept_0 + got.astype(F32), to_x, to_y))
+        qkv_sum_0 = kept_0 + chips(sent, 2, n_vox).astype(F32)
+        kept_1, sent = groups_of(left + end_y.astype(F32), right + end_x.astype(F32), 1)
+        kept_1, sent = halves_of(kept_1 + chips(sent, 1, n_vox).astype(F32))
+        kept_1 = kept_1 + chips(sent, 2, n_vox).astype(F32)
+        height = normed.shape[1] // 4
+        qkv_sums = [qkv_sum_0, kept_1[:height]]
+        out_sum = kept_1[height:]
+    else:
+        out_sums = [out_grad_0, out_grad_1]
+        qkv_sums = [dot(normed, grad, ((0,), (0,))) for grad in (grad_0, grad_1)]
+        ngrad_part = dot(grad_0, weights_0, ((1,), (1,))) + dot(grad_1, weights_1, ((1,), (1,)))
+
     scale_parts = {}
-    qkv_sums, out_sums = [], []
-    for chunk, pairs in enumerate(CHUNKS):
-        chunk_scales = jnp.concatenate([scales[2 * p : 2 * p + 2] for p in pairs])
-        att, dq, dk, dv, rim_b, rim_a, ds = attention(
-            packed_chunks[chunk], *halos[chunk], upstream, mult, valid, chunk_scales, pairs
-        )
-        back_a = lax.ppermute(rim_b, "vox", down).astype(F32)
-        back_b = lax.ppermute(rim_a, "vox", up).astype(F32)
-        head_sums_of = jnp.sum(ds.reshape(-1, 8, 2, PAIR), axis=(1, 3))
+    for pairs, result in zip(CHUNKS, (first, second)):
+        sums = jnp.sum(result[6].reshape(2, 8, 2, PAIR), axis=(1, 3))
         for i, p in enumerate(pairs):
-            scale_parts[p] = head_sums_of[i]
-
-        out_rows = jnp.concatenate([out_half[p * PAIR : (p + 1) * PAIR] for p in pairs], axis=0)
-        mixed_part = mixed_part + dot(att, out_rows)
-        out_grad = dot(att, chip_cotangent, ((0,), (0,)))
-
-        def with_rims(grad, index):
-            return jnp.concatenate(
-                [
-                    grad[:margin] + back_b[index],
-                    grad[margin : rows - margin],
-                    grad[rows - margin :] + back_a[index],
-                ],
-                axis=0,
-            ).astype(BF)
-
-        grad_packed = jnp.concatenate([dq, with_rims(dk, 0), with_rims(dv, 1)], axis=1)
-        ngrad_part = ngrad_part + dot(grad_packed, qkv_chunks[chunk], ((1,), (1,)))
-        if fast:
-            even, low = chip % 2 == 0, chip < 2
-            quarter = model_width // 4
-            cols = [out_grad[:, k * quarter : (k + 1) * quarter] for k in range(4)]
-            kept = [jnp.where(even, cols[k], cols[k + 1]) for k in (0, 2)]
-            sent = [jnp.where(even, cols[k + 1], cols[k]) for k in (0, 2)]
-            got = chips(jnp.concatenate(sent, axis=1).astype(BF), 1, n_vox).astype(F32)
-            kept = [kept[0] + got[:, :quarter], kept[1] + got[:, quarter:]]
-            got = chips(jnp.where(low, kept[1], kept[0]).astype(BF), 2, n_vox).astype(F32)
-            out_sums.append(jnp.where(low, kept[0], kept[1]) + got)
-
-            part = reduce_square(normed_blocks, grad_packed)
-            groups = [part[:, k * PAIR : (k + 1) * PAIR] for k in range(6)]
-            sets = ((0, 3, 4), (1, 2, 5)) if chunk == 0 else ((0, 1, 3), (2, 4, 5))
-            evens, odds = [jnp.concatenate([groups[k] for k in s], axis=1) for s in sets]
-            got = chips(jnp.where(even, odds, evens).astype(BF), 1, n_vox).astype(F32)
-            kept = jnp.where(even, evens, odds) + got
-            left, right = kept[:, : 2 * PAIR], kept[:, PAIR:]
-            got = chips(jnp.where(low, right, left).astype(BF), 2, n_vox).astype(F32)
-            qkv_sums.append(jnp.where(low, left, right) + got)
-        else:
-            out_sums.append(out_grad)
-            qkv_sums.append(dot(normed, grad_packed, ((0,), (0,))))
+            scale_parts[p] = sums[i]
 
     mixed_mine = lax.dynamic_slice_in_dim(mixed_part, core * own_rows, own_rows, 0)
     mixed_theirs = lax.dynamic_slice_in_dim(mixed_part, (1 - core) * own_rows, own_rows, 0)
@@ -497,24 +630,14 @@
     scale_grad = spread_groups(scale_part, 0, group_heads, core)
     if fast:
         small = jnp.concatenate([gain_grad, scale_grad, jnp.zeros((112,), F32)]).reshape(9, 128)
-        for step in (1, 2):
-            small = small + square(small, step)
-        for step in (1, 2, 4):
-            small = small + lax.ppermute(small, "vox", [(i, i ^ step) for i in range(n_vox)])
+        every = lax.all_gather(small, ("vox", "fsdp"), axis=0, tiled=False)
+        small = jnp.sum(every, axis=0)
         small = small.reshape(-1)
         summed_gain, summed_scale = small[:model_width], small[model_width : model_width + HEADS]
     else:
         summed_gain, summed_scale = lax.psum((gain_grad, scale_grad), ("vox", "fsdp"))
 
     if fast:
-        by_pair = {}
-        for pairs, total in zip(CHUNKS, out_sums):
-            for i, p in enumerate(pairs):
-                by_pair[p] = total[i * PAIR : (i + 1) * PAIR]
-        turned = xor_blocks([by_pair[p] for p in range(4)], scene)
-        out_sum = turned[0]
-        for step in (1, 2, 3):
-            out_sum = out_sum + square(turned[step].astype(BF), step).astype(F32)
         half = out_sum.shape[1] // 2
         first, second = out_sum[:, :half], out_sum[:, half:]
         out_other = lax.ppermute(jnp.where(core == 0, second, first), "vox", swap)

time: 246 us -> 272 us (1.11)
  blocking collectives: 0 us -> 72.1 us
  waiting for transfers between devices: 80.6 us -> 37.1 us
  starting transfers between devices: 62.8 us -> 42.7 us
  between operations: 2.14 us -> 15.3 us
  matrix products: 19.8 us -> 25.2 us
  other arithmetic: 30.8 us -> 27.8 us
    all_gather x0 -> x1, blocking collectives: none -> 72.1 us  [on_device(): every = lax.all_gather(small, ('vox', 'fsdp'), axis=0, tiled=False)]
    ppermute x25 -> x12, waiting for transfers between devices: 51.9 us -> 23.2 us  [square(): return lax.ppermute(value, 'fsdp', [(i, i ^ step) for i in range(4)])]
    ppermute x8 -> x4, waiting for transfers between devices: 21 us -> 11.2 us  [chips(): return lax.ppermute(value, 'vox', [(i, i ^ 2 * step) for i in range(n_vox)])]
    ppermute x11 -> x8, starting transfers between devices: 25.8 us -> 16.4 us  [the longest x4 13 us: pairings(): lax.ppermute(first, 'vox', near_chips)]
    ppermute x25 -> x12, starting transfers between devices: 24.7 us -> 15.6 us  [square(): return lax.ppermute(value, 'fsdp', [(i, i ^ step) for i in range(4)])]
    unnamed x13 -> x0, other arithmetic: 9.03 us -> none
    dot_general x21, matrix products: 19.8 us -> 25.2 us  [dot(): return lax.dot_general(a, b, (dims, ((), ())), preferred_element_type=F32)]
    ppermute x11 -> x8, waiting for transfers between devices: 6.66 us -> 2.61 us  [the longest x4 2.59 us: pairings(): lax.ppermute(first, 'vox', near_chips)]
  transfers between devices with their start and end apart: 51 -> 32, of which waited for: 25 -> 8; matrix products, arithmetic and copies ran while one was open for 21% -> 21% of each run, Pallas kernels for 13% -> 11%
where the time goes in v3:
time: 272 us; the launch traced here: 271 us
  blocking collectives  72.1 us (27%)
  starting transfers between devices  42.7 us (16%)
  waiting for transfers between devices  37.1 us (14%)
  Pallas kernels  32.1 us (12%)
  other arithmetic  27.8 us (10%)
  matrix products  25.2 us (9%)
  local copies, waits for them, and re-layouts  18.8 us (7%)
  between operations  15.3 us (6%)
    all_gather x1, blocking collectives, on_device(): every = lax.all_gather(small, ('vox', 'fsdp'), axis=0, tiled=False)  72.1 us
    pallas_call x2, Pallas kernels, attention(): pl.pallas_call(attention_kernel, grid_spec=pltpu.PrefetchScalarGridSpec(n...  31.1 us
    dot_general x21, matrix products, dot(): return lax.dot_general(a, b, (dims, ((), ())), preferred_element_type=F32)  25.2 us
    ppermute x12, waiting for transfers between devices, square(): return lax.ppermute(value, 'fsdp', [(i, i ^ step) for i in range(4)])  23.2 us
    ppermute x12, starting transfers between devices, square(): return lax.ppermute(value, 'fsdp', [(i, i ^ step) for i in range(4)])  15.6 us
    ppermute x4, starting transfers between devices, pairings(): lax.ppermute(first, 'vox', near_chips)  13 us
    ppermute x4, waiting for transfers between devices, chips(): return lax.ppermute(value, 'vox', [(i, i ^ 2 * step) for i in range(n_vox)])  11.2 us
    unnamed x132, local copies, waits for them, and re-layouts  9.2 us
  transfers between devices with their start and end apart: 32, of which 8 were waited for; matrix products, arithmetic and copies ran while one was open for 21% of the time, Pallas kernels for 11%

profile of v3, /device:TPU:0, one launch (start us, length us, event | category | flops | bytes accessed | tf_op | source)
XLA Modules:
  0.0 271.1 jit_solution(14828897593530461541)
XLA Ops:
  10.7 3.0 %collective-permute-start.3 = (bf16[256,1280]{1,0:T(8,128)(2,1)S(1)}, bf16[256,1280]{1,0:T(8,128)(2,1)S(1)}, u32[]{:S(2)}, u32[]{:S(2)}) collective-permute-start(bf16[256,1280]{1,0:T(8,128)(2,1)S(1)} %get-tuple-element.32), channel_id=1, source_target_pairs={{0,2},{1,3},{2,0},{3,1},{4,6},{5,7},{6,4},{7,5},{8,10},{9,11},{10,... | collective-permute-start | bytes 1966088 | tf_op jit(solution)/shard_map/ppermute | solution.py:335
  18.8 9.5 %collective-permute-done.3 = bf16[256,1280]{1,0:T(8,128)(2,1)S(1)} collective-permute-done((bf16[256,1280]{1,0:T(8,128)(2,1)S(1)}, bf16[256,1280]{1,0:T(8,128)(2,1)S(1)}, u32[]{:S(2)}, u32[]{:S(2)}) %collective-permute-start.3) | collective-permute-done | bytes 655392 | tf_op jit(solution)/shard_map/ppermute | solution.py:335
  28.4 1.8 collective-permute-start.4
  31.2 1.6 collective-permute-start.5
  37.7 1.8 broadcast_select_fusion.1
  41.8 2.3 convolution_convert_fusion.1.q_ref.k_ref.v_ref
  45.0 4.4 %collective-permute-start.6 = (bf16[192,512]{1,0:T(8,128)(2,1)S(1)}, bf16[192,512]{1,0:T(8,128)(2,1)S(1)}, u32[]{:S(2)}, u32[]{:S(2)}) collective-permute-start(bf16[192,512]{1,0:T(8,128)(2,1)S(1)} %get-tuple-element.95), channel_id=1, source_target_pairs={{0,8},{4,12},{8,0},{12,4},{16,24},{20,28},{24,16},{28,20},{1,9},{5... | collective-permute-start | bytes 589832 | tf_op jit(solution)/shard_map/ppermute | solution.py:490
  50.5 2.6 collective-permute-done.6.k1_ref.v1_ref
  53.1 15.5 %block_attention.2 = (bf16[768,256]{1,0:T(8,128)(2,1)S(1)}, bf16[768,256]{1,0:T(8,128)(2,1)S(1)}, f32[768,256]{1,0:T(8,128)S(1)}, f32[768,256]{1,0:T(8,128)S(1)}...) custom-call(s32[12,8]{1,0:T(8,128)S(1)} %copy.31.mult_ref, ...), custom_call_target="tpu_custom_call" | custom-call | flops 19327352832 | bytes 3932160 | tf_op jit(solution)/shard_map/block_attention/pallas_call | solution.py:189
  70.9 3.8 %collective-permute-start.10 = (bf16[2,192,256]{2,1,0:T(8,128)(2,1)S(1)}, bf16[2,192,256]{2,1,0:T(8,128)(2,1)S(1)}, u32[]{:S(2)}, u32[]{:S(2)}) collective-permute-start(bf16[2,192,256]{2,1,0:T(8,128)(2,1)S(1)} %get-tuple-element.36), channel_id=1, source_target_pairs={{0,8},{4,12},{8,0},{12,4},{16,24},{20,28},{24,16},{28,20},{1,9},{5... | collective-permute-start | bytes 589832 | tf_op jit(solution)/shard_map/ppermute | solution.py:490
  74.7 3.0 %fusion.76 = f32[256,1024]{1,0:T(8,128)} fusion(bf16[768,256]{1,0:T(8,128)(2,1)S(1)} %get-tuple-element.41, bf16[384,1024]{1,0:T(8,128)(2,1)} %copy-done.11, bf16[384,1024]{1,0:T(8,128)(2,1)} %copy-done.9), kind=kOutput, calls=%fused_computation.139 | convolution fusion | flops 405798912 | bytes 3014656 | tf_op jit(solution)/shard_map/dot_general | solution.py:22
  77.7 2.2 fusion.52
  88.5 2.9 %collective-permute-start.11 = (bf16[192,512]{1,0:T(8,128)(2,1)S(1)}, bf16[192,512]{1,0:T(8,128)(2,1)S(1)}, u32[]{:S(2)}, u32[]{:S(2)}) collective-permute-start(bf16[192,512]{1,0:T(8,128)(2,1)S(1)} %get-tuple-element.89), channel_id=1, source_target_pairs={{0,8},{4,12},{8,0},{12,4},{16,24},{20,28},{24,16},{28,20},{1,9},{5... | collective-permute-start | bytes 589832 | tf_op jit(solution)/shard_map/ppermute | solution.py:490
  95.2 15.6 %block_attention.3 = (bf16[768,256]{1,0:T(8,128)(2,1)S(1)}, bf16[768,256]{1,0:T(8,128)(2,1)S(1)}, f32[768,256]{1,0:T(8,128)S(1)}, f32[768,256]{1,0:T(8,128)S(1)}...) custom-call(s32[12,8]{1,0:T(8,128)S(1)} %copy.31.mult_ref, ...), custom_call_target="tpu_custom_call" | custom-call | flops 19327352832 | bytes 3932160 | tf_op jit(solution)/shard_map/block_attention/pallas_call | solution.py:189
  114.1 1.9 collective-permute-start.18
  117.0 1.6 fusion.69
  120.3 1.5 add_convert_fusion
  121.9 1.5 collective-permute-start.16
  129.6 1.6 collective-permute-done.14
  137.7 2.1 collective-permute-start.27
  139.8 2.3 convolution_add_fusion.1
  142.6 7.3 %collective-permute-done.23 = bf16[512,640]{1,0:T(8,128)(2,1)S(1)} collective-permute-done((bf16[512,640]{1,0:T(8,128)(2,1)S(1)}, bf16[512,640]{1,0:T(8,128)(2,1)S(1)}, u32[]{:S(2)}, u32[]{:S(2)}) %collective-permute-start.23) | collective-permute-done | bytes 655392 | tf_op jit(solution)/shard_map/ppermute | solution.py:335
  150.6 1.5 collective-permute-start.22
  152.8 4.3 %collective-permute-done.24 = bf16[256,640]{1,0:T(8,128)(2,1)S(1)} collective-permute-done((bf16[256,640]{1,0:T(8,128)(2,1)S(1)}, bf16[256,640]{1,0:T(8,128)(2,1)S(1)}, u32[]{:S(2)}, u32[]{:S(2)}) %collective-permute-start.24) | collective-permute-done | bytes 327712 | tf_op jit(solution)/shard_map/ppermute | solution.py:335
  158.0 2.1 collective-permute-start.25
  161.4 5.5 %collective-permute-done.25 = bf16[256,640]{1,0:T(8,128)(2,1)S(1)} collective-permute-done((bf16[256,640]{1,0:T(8,128)(2,1)S(1)}, bf16[256,640]{1,0:T(8,128)(2,1)S(1)}, u32[]{:S(2)}, u32[]{:S(2)}) %collective-permute-start.25) | collective-permute-done | bytes 327712 | tf_op jit(solution)/shard_map/ppermute | solution.py:350
  167.1 3.6 %collective-permute-start.26 = (bf16[384,256]{1,0:T(8,128)(2,1)S(1)}, bf16[384,256]{1,0:T(8,128)(2,1)S(1)}, u32[]{:S(2)}, u32[]{:S(2)}) collective-permute-start(bf16[384,256]{1,0:T(8,128)(2,1)S(1)} %select_convert_fusion.2), channel_id=1, source_target_pairs={{0,16},{4,20},{8,24},{12,28},{16,0},{20,4},{24,8},{28,12},{1,17},{... | collective-permute-start | bytes 589832 | tf_op jit(solution)/shard_map/ppermute | solution.py:350
  170.7 5.7 %collective-permute-done.26 = bf16[384,256]{1,0:T(8,128)(2,1)S(1)} collective-permute-done((bf16[384,256]{1,0:T(8,128)(2,1)S(1)}, bf16[384,256]{1,0:T(8,128)(2,1)S(1)}, u32[]{:S(2)}, u32[]{:S(2)}) %collective-permute-start.26) | collective-permute-done | bytes 196640 | tf_op jit(solution)/shard_map/ppermute | solution.py:350
  181.2 2.0 fusion.7
  184.6 72.1 %all_gather.7 = f32[32,9,128]{2,1,0:T(8,128)} all-gather(f32[1,9,128]{2,1,0:T(8,128)S(1)} %bitcast.117), channel_id=1, replica_groups=mesh['vox'=8,'fsdp'=4] {'vox','fsdp'}, dimensions={0}, use_global_device_ids=true | all-gather | bytes 152064 | tf_op jit(solution)/shard_map/all_gather | solution.py:633
  257.7 2.2 fusion.14
  262.5 1.7 pad_maximum_fusion.51
  (298 shorter events, 65.3 us)
Async XLA Ops:
  7.2 75.8 %all-gather.2.cloned.1.call-start = ((), (), s32[]{:S(2)}) async-start(), calls=%async_computation | async-start | bytes 1966080 | tf_op jit(solution)/shard_map/all_gather | solution.py:437
  10.7 17.7 %collective-permute-start.3 = (bf16[256,1280]{1,0:T(8,128)(2,1)S(1)}, bf16[256,1280]{1,0:T(8,128)(2,1)S(1)}, u32[]{:S(2)}, u32[]{:S(2)}) collective-permute-start(bf16[256,1280]{1,0:T(8,128)(2,1)S(1)} %get-tuple-element.32), channel_id=1, source_target_pairs={{0,2},{1,3},{2,0},{3,1},{4,6},{5,7},{6,4},{7,5},{8,10},{9,11},{10,... | collective-permute-start | bytes 1966088 | tf_op jit(solution)/shard_map/ppermute | solution.py:335
  13.6 16.5 %collective-permute-start.2 = (bf16[256,1280]{1,0:T(8,128)(2,1)S(1)}, bf16[256,1280]{1,0:T(8,128)(2,1)}, u32[]{:S(2)}, u32[]{:S(2)}) collective-permute-start(bf16[256,1280]{1,0:T(8,128)(2,1)S(1)} %get-tuple-element.32), channel_id=1, source_target_pairs={{0,1},{1,0},{2,3},{3,2},{4,5},{5,4},{6,7},{7,6},{8,9},{9,8},{10,11... | collective-permute-start | bytes 1966088 | tf_op jit(solution)/shard_map/ppermute | solution.py:335
  15.2 3.3 %collective-permute-start.1 = (f32[6,9]{0,1:T(8,128)S(1)}, f32[6,9]{0,1:T(8,128)S(1)}, u32[]{:S(2)}, u32[]{:S(2)}) collective-permute-start(f32[6,9]{0,1:T(8,128)S(1)} %fusion.106), channel_id=1, source_target_pairs={{0,4},{4,0},{8,12},{12,8},{16,20},{20,16},{24,28},{28,24},{1,5},{5... | collective-permute-start | bytes 656 | tf_op jit(solution)/shard_map/ppermute | solution.py:460
  15.3 19.8 %collective-permute-start = (bf16[384,1024]{1,0:T(8,128)(2,1)S(1)}, bf16[384,1024]{1,0:T(8,128)(2,1)}, u32[]{:S(2)}, u32[]{:S(2)}) collective-permute-start(bf16[384,1024]{1,0:T(8,128)(2,1)S(1)} %bitcast.109), channel_id=1, source_target_pairs={{0,4},{4,0},{8,12},{12,8},{16,20},{20,16},{24,28},{28,24},{1,5},{5... | collective-permute-start | bytes 2359304 | tf_op jit(solution)/shard_map/ppermute | solution.py:456
  15.8 21.9 %collective-permute-start.8 = (bf16[384,1024]{1,0:T(8,128)(2,1)S(1)}, bf16[384,1024]{1,0:T(8,128)(2,1)}, u32[]{:S(2)}, u32[]{:S(2)}) collective-permute-start(bf16[384,1024]{1,0:T(8,128)(2,1)S(1)} %bitcast.114), channel_id=1, source_target_pairs={{0,4},{4,0},{8,12},{12,8},{16,20},{20,16},{24,28},{28,24},{1,5},{5... | collective-permute-start | bytes 2359304 | tf_op jit(solution)/shard_map/ppermute | solution.py:457
  28.4 11.2 %collective-permute-start.4 = (bf16[128,1280]{1,0:T(8,128)(2,1)S(1)}, bf16[128,1280]{1,0:T(8,128)(2,1)}, u32[]{:S(2)}, u32[]{:S(2)}) collective-permute-start(bf16[128,1280]{1,0:T(8,128)(2,1)S(1)} %slice.486), channel_id=1, source_target_pairs={{0,1},{1,0},{2,3},{3,2},{4,5},{5,4},{6,7},{7,6},{8,9},{9,8},{10,11... | collective-permute-start | bytes 983048 | tf_op jit(solution)/shard_map/ppermute | solution.py:335
  31.2 9.4 %collective-permute-start.5 = (bf16[128,1280]{1,0:T(8,128)(2,1)S(1)}, bf16[128,1280]{1,0:T(8,128)(2,1)S(1)}, u32[]{:S(2)}, u32[]{:S(2)}) collective-permute-start(bf16[128,1280]{1,0:T(8,128)(2,1)S(1)} %slice.487), channel_id=1, source_target_pairs={{0,2},{1,3},{2,0},{3,1},{4,6},{5,7},{6,4},{7,5},{8,10},{9,11},{10,... | collective-permute-start | bytes 983048 | tf_op jit(solution)/shard_map/ppermute | solution.py:335
  44.1 6.4 %collective-permute-start.7 = (bf16[192,512]{1,0:T(8,128)(2,1)S(1)}, bf16[192,512]{1,0:T(8,128)(2,1)S(1)}, u32[]{:S(2)}, u32[]{:S(2)}) collective-permute-start(bf16[192,512]{1,0:T(8,128)(2,1)S(1)} %get-tuple-element.94), channel_id=1, source_target_pairs={{0,0},{4,4},{8,16},{12,20},{16,8},{20,12},{24,24},{28,28},{1,1},{5... | collective-permute-start | bytes 589832 | tf_op jit(solution)/shard_map/ppermute | solution.py:490
  45.0 8.1 %collective-permute-start.6 = (bf16[192,512]{1,0:T(8,128)(2,1)S(1)}, bf16[192,512]{1,0:T(8,128)(2,1)S(1)}, u32[]{:S(2)}, u32[]{:S(2)}) collective-permute-start(bf16[192,512]{1,0:T(8,128)(2,1)S(1)} %get-tuple-element.95), channel_id=1, source_target_pairs={{0,8},{4,12},{8,0},{12,4},{16,24},{20,28},{24,16},{28,20},{1,9},{5... | collective-permute-start | bytes 589832 | tf_op jit(solution)/shard_map/ppermute | solution.py:490
  70.1 10.4 %collective-permute-start.9 = (bf16[2,192,256]{2,1,0:T(8,128)(2,1)S(1)}, bf16[2,192,256]{2,1,0:T(8,128)(2,1)S(1)}, u32[]{:S(2)}, u32[]{:S(2)}) collective-permute-start(bf16[2,192,256]{2,1,0:T(8,128)(2,1)S(1)} %get-tuple-element.35), channel_id=1, source_target_pairs={{0,0},{4,4},{8,16},{12,20},{16,8},{20,12},{24,24},{28,28},{1,1},{5... | collective-permute-start | bytes 589832 | tf_op jit(solution)/shard_map/ppermute | solution.py:490
  70.9 9.6 %collective-permute-start.10 = (bf16[2,192,256]{2,1,0:T(8,128)(2,1)S(1)}, bf16[2,192,256]{2,1,0:T(8,128)(2,1)S(1)}, u32[]{:S(2)}, u32[]{:S(2)}) collective-permute-start(bf16[2,192,256]{2,1,0:T(8,128)(2,1)S(1)} %get-tuple-element.36), channel_id=1, source_target_pairs={{0,8},{4,12},{8,0},{12,4},{16,24},{20,28},{24,16},{28,20},{1,9},{5... | collective-permute-start | bytes 589832 | tf_op jit(solution)/shard_map/ppermute | solution.py:490
  82.4 41.6 %collective-permute-start.13 = (bf16[512,384]{1,0:T(8,128)(2,1)}, bf16[512,384]{1,0:T(8,128)(2,1)}, u32[]{:S(2)}, u32[]{:S(2)}) collective-permute-start(bf16[512,384]{1,0:T(8,128)(2,1)} %convolution_convert_fusion.6), channel_id=1, source_target_pairs={{0,1},{1,0},{2,3},{3,2},{4,5},{5,4},{6,7},{7,6},{8,9},{9,8},{10,11... | collective-permute-start | bytes 1179656 | tf_op jit(solution)/shard_map/ppermute | solution.py:335
  87.6 7.6 %collective-permute-start.12 = (bf16[192,512]{1,0:T(8,128)(2,1)S(1)}, bf16[192,512]{1,0:T(8,128)(2,1)S(1)}, u32[]{:S(2)}, u32[]{:S(2)}) collective-permute-start(bf16[192,512]{1,0:T(8,128)(2,1)S(1)} %get-tuple-element.88), channel_id=1, source_target_pairs={{0,0},{4,4},{8,16},{12,20},{16,8},{20,12},{24,24},{28,28},{1,1},{5... | collective-permute-start | bytes 589832 | tf_op jit(solution)/shard_map/ppermute | solution.py:490
  88.5 6.7 %collective-permute-start.11 = (bf16[192,512]{1,0:T(8,128)(2,1)S(1)}, bf16[192,512]{1,0:T(8,128)(2,1)S(1)}, u32[]{:S(2)}, u32[]{:S(2)}) collective-permute-start(bf16[192,512]{1,0:T(8,128)(2,1)S(1)} %get-tuple-element.89), channel_id=1, source_target_pairs={{0,8},{4,12},{8,0},{12,4},{16,24},{20,28},{24,16},{28,20},{1,9},{5... | collective-permute-start | bytes 589832 | tf_op jit(solution)/shard_map/ppermute | solution.py:490
  92.8 27.5 %collective-permute-start.15 = (bf16[512,384]{1,0:T(8,128)(2,1)}, bf16[512,384]{1,0:T(8,128)(2,1)}, u32[]{:S(2)}, u32[]{:S(2)}) collective-permute-start(bf16[512,384]{1,0:T(8,128)(2,1)} %convolution_convert_fusion.5), channel_id=1, source_target_pairs={{0,2},{1,3},{2,0},{3,1},{4,6},{5,7},{6,4},{7,5},{8,10},{9,11},{10,... | collective-permute-start | bytes 1179656 | tf_op jit(solution)/shard_map/ppermute | solution.py:335
  114.1 12.6 %collective-permute-start.18 = (bf16[2,192,256]{2,1,0:T(8,128)(2,1)S(1)}, bf16[2,192,256]{2,1,0:T(8,128)(2,1)S(1)}, u32[]{:S(2)}, u32[]{:S(2)}) collective-permute-start(bf16[2,192,256]{2,1,0:T(8,128)(2,1)S(1)} %get-tuple-element.43), channel_id=1, source_target_pairs={{0,8},{4,12},{8,0},{12,4},{16,24},{20,28},{24,16},{28,20},{1,9},{5... | collective-permute-start | bytes 589832 | tf_op jit(solution)/shard_map/ppermute | solution.py:490
  116.0 10.8 %collective-permute-start.17 = (bf16[2,192,256]{2,1,0:T(8,128)(2,1)S(1)}, bf16[2,192,256]{2,1,0:T(8,128)(2,1)S(1)}, u32[]{:S(2)}, u32[]{:S(2)}) collective-permute-start(bf16[2,192,256]{2,1,0:T(8,128)(2,1)S(1)} %get-tuple-element.44), channel_id=1, source_target_pairs={{0,0},{4,4},{8,16},{12,20},{16,8},{20,12},{24,24},{28,28},{1,1},{5... | collective-permute-start | bytes 589832 | tf_op jit(solution)/shard_map/ppermute | solution.py:490
  121.9 6.5 %collective-permute-start.16 = (bf16[256,384]{1,0:T(8,128)(2,1)S(1)}, bf16[256,384]{1,0:T(8,128)(2,1)S(1)}, u32[]{:S(2)}, u32[]{:S(2)}) collective-permute-start(bf16[256,384]{1,0:T(8,128)(2,1)S(1)} %add_convert_fusion), channel_id=1, source_target_pairs={{0,1},{1,0},{2,3},{3,2},{4,5},{5,4},{6,7},{7,6},{8,9},{9,8},{10,11... | collective-permute-start | bytes 589832 | tf_op jit(solution)/shard_map/ppermute | solution.py:335
  125.4 5.7 %collective-permute-start.14 = (bf16[256,384]{1,0:T(8,128)(2,1)S(1)}, bf16[256,384]{1,0:T(8,128)(2,1)S(1)}, u32[]{:S(2)}, u32[]{:S(2)}) collective-permute-start(bf16[256,384]{1,0:T(8,128)(2,1)S(1)} %add_convert_fusion.1), channel_id=1, source_target_pairs={{0,2},{1,3},{2,0},{3,1},{4,6},{5,7},{6,4},{7,5},{8,10},{9,11},{10,... | collective-permute-start | bytes 589832 | tf_op jit(solution)/shard_map/ppermute | solution.py:335
  135.8 14.2 %collective-permute-start.23 = (bf16[512,640]{1,0:T(8,128)(2,1)S(1)}, bf16[512,640]{1,0:T(8,128)(2,1)S(1)}, u32[]{:S(2)}, u32[]{:S(2)}) collective-permute-start(bf16[512,640]{1,0:T(8,128)(2,1)S(1)} %get-tuple-element.129), channel_id=1, source_target_pairs={{0,2},{1,3},{2,0},{3,1},{4,6},{5,7},{6,4},{7,5},{8,10},{9,11},{10,... | collective-permute-start | bytes 1966088 | tf_op jit(solution)/shard_map/ppermute | solution.py:335
  136.4 14.1 %collective-permute-start.21 = (bf16[512,640]{1,0:T(8,128)(2,1)S(1)}, bf16[512,640]{1,0:T(8,128)(2,1)S(1)}, u32[]{:S(2)}, u32[]{:S(2)}) collective-permute-start(bf16[512,640]{1,0:T(8,128)(2,1)S(1)} %get-tuple-element.130), channel_id=1, source_target_pairs={{0,1},{1,0},{2,3},{3,2},{4,5},{5,4},{6,7},{7,6},{8,9},{9,8},{10,11... | collective-permute-start | bytes 1966088 | tf_op jit(solution)/shard_map/ppermute | solution.py:335
  137.7 22.5 %collective-permute-start.27 = (bf16[256,384]{1,0:T(8,128)(2,1)S(1)}, bf16[256,384]{1,0:T(8,128)(2,1)S(1)}, u32[]{:S(2)}, u32[]{:S(2)}) collective-permute-start(bf16[256,384]{1,0:T(8,128)(2,1)S(1)} %select_convert_fusion.1), channel_id=1, source_target_pairs={{0,8},{4,12},{8,0},{12,4},{16,24},{20,28},{24,16},{28,20},{1,9},{5... | collective-permute-start | bytes 589832 | tf_op jit(solution)/shard_map/ppermute | solution.py:350
  150.0 7.1 %collective-permute-start.24 = (bf16[256,640]{1,0:T(8,128)(2,1)S(1)}, bf16[256,640]{1,0:T(8,128)(2,1)S(1)}, u32[]{:S(2)}, u32[]{:S(2)}) collective-permute-start(bf16[256,640]{1,0:T(8,128)(2,1)S(1)} %fusion.33), channel_id=1, source_target_pairs={{0,1},{1,0},{2,3},{3,2},{4,5},{5,4},{6,7},{7,6},{8,9},{9,8},{10,11... | collective-permute-start | bytes 983048 | tf_op jit(solution)/shard_map/ppermute | solution.py:335
  150.6 7.1 %collective-permute-start.22 = (bf16[256,640]{1,0:T(8,128)(2,1)S(1)}, bf16[256,640]{1,0:T(8,128)(2,1)S(1)}, u32[]{:S(2)}, u32[]{:S(2)}) collective-permute-start(bf16[256,640]{1,0:T(8,128)(2,1)S(1)} %fusion.39), channel_id=1, source_target_pairs={{0,2},{1,3},{2,0},{3,1},{4,6},{5,7},{6,4},{7,5},{8,10},{9,11},{10,... | collective-permute-start | bytes 983048 | tf_op jit(solution)/shard_map/ppermute | solution.py:335
  152.2 27.9 %collective-permute-start.19 = (f32[384,1024]{1,0:T(8,128)S(1)}, f32[384,1024]{1,0:T(8,128)S(1)}, u32[]{:S(2)}, u32[]{:S(2)}) collective-permute-start(f32[384,1024]{1,0:T(8,128)S(1)} %constant_dynamic-slice_fusion.1), channel_id=1, source_target_pairs={{0,4},{4,0},{8,12},{12,8},{16,20},{20,16},{24,28},{28,24},{1,5},{5... | collective-permute-start | bytes 4718600 | tf_op jit(solution)/shard_map/ppermute | solution.py:605
  152.3 27.4 %collective-permute-start.20 = (f32[384,1024]{1,0:T(8,128)S(1)}, f32[384,1024]{1,0:T(8,128)S(1)}, u32[]{:S(2)}, u32[]{:S(2)}) collective-permute-start(f32[384,1024]{1,0:T(8,128)S(1)} %constant_dynamic-slice_fusion), channel_id=1, source_target_pairs={{0,4},{4,0},{8,12},{12,8},{16,20},{20,16},{24,28},{28,24},{1,5},{5... | collective-permute-start | bytes 4718600 | tf_op jit(solution)/shard_map/ppermute | solution.py:610
  158.0 8.8 %collective-permute-start.25 = (bf16[256,640]{1,0:T(8,128)(2,1)S(1)}, bf16[256,640]{1,0:T(8,128)(2,1)S(1)}, u32[]{:S(2)}, u32[]{:S(2)}) collective-permute-start(bf16[256,640]{1,0:T(8,128)(2,1)S(1)} %select_convert_fusion), channel_id=1, source_target_pairs={{0,8},{4,12},{8,0},{12,4},{16,24},{20,28},{24,16},{28,20},{1,9},{5... | collective-permute-start | bytes 983048 | tf_op jit(solution)/shard_map/ppermute | solution.py:350
  160.3 10.4 %collective-permute-start.28 = (bf16[256,256]{1,0:T(8,128)(2,1)S(1)}, bf16[256,256]{1,0:T(8,128)(2,1)S(1)}, u32[]{:S(2)}, u32[]{:S(2)}) collective-permute-start(bf16[256,256]{1,0:T(8,128)(2,1)S(1)} %select_convert_fusion.3), channel_id=1, source_target_pairs={{0,16},{4,20},{8,24},{12,28},{16,0},{20,4},{24,8},{28,12},{1,17},{... | collective-permute-start | bytes 393224 | tf_op jit(solution)/shard_map/ppermute | solution.py:350
  167.1 9.4 %collective-permute-start.26 = (bf16[384,256]{1,0:T(8,128)(2,1)S(1)}, bf16[384,256]{1,0:T(8,128)(2,1)S(1)}, u32[]{:S(2)}, u32[]{:S(2)}) collective-permute-start(bf16[384,256]{1,0:T(8,128)(2,1)S(1)} %select_convert_fusion.2), channel_id=1, source_target_pairs={{0,16},{4,20},{8,24},{12,28},{16,0},{20,4},{24,8},{28,12},{1,17},{... | collective-permute-start | bytes 589832 | tf_op jit(solution)/shard_map/ppermute | solution.py:350
  177.2 83.8 %collective-permute-start.30 = (f32[128,128]{1,0:T(8,128)}, f32[128,128]{1,0:T(8,128)}, u32[]{:S(2)}, u32[]{:S(2)}) collective-permute-start(f32[128,128]{1,0:T(8,128)} %slice_select_fusion.8), channel_id=1, source_target_pairs={{0,4},{4,0},{8,12},{12,8},{16,20},{20,16},{24,28},{28,24},{1,5},{5... | collective-permute-start | bytes 196616 | tf_op jit(solution)/shard_map/ppermute | solution.py:643
  178.6 84.0 %collective-permute-start.29 = (f32[256,128]{1,0:T(8,128)}, f32[256,128]{1,0:T(8,128)}, u32[]{:S(2)}, u32[]{:S(2)}) collective-permute-start(f32[256,128]{1,0:T(8,128)} %get-tuple-element.63), channel_id=1, source_target_pairs={{0,4},{4,0},{8,12},{12,8},{16,20},{20,16},{24,28},{28,24},{1,5},{5... | collective-permute-start | bytes 393224 | tf_op jit(solution)/shard_map/ppermute | solution.py:658
  (66 other events, 369.8 us)
Sparse Core Ops, SparseCore 0:
  30.3 31.2 all-gather.1
